TPU v7x, 128 devices: a whole 4x4x4 slice. The times are simulated.
128 devices in a mesh: zc: 16 (over y, z), zl: 8 (over x, core).
Axes of the slice: x: 4, y: 4, z: 4, core: 2. Of those that a mesh axis runs over, the one named last changes fastest.
Arguments:
- velocity: float32 [8192, 3, 1536], P(('zc', 'zl')), may hold values from -6 to 6
- base_flow: float32 [192], replicated, may hold values from 0.5 to 1.5
- slot_mask: int32 [8, 8192], P(None, ('zc', 'zl')), may hold values 0 or 1
Outputs:
- new_velocity: float32 [8192, 3, 1536], P(('zc', 'zl'))
All inputs are finite; a program needn't handle non-finite values. No bound on the sum of `slot_mask` on one device may be relied on, other than what follows from the above.
Results may differ from a plain program's by a relative error of at most 0.0003.
Values sent between devices are 32-bit elements; how exact they have to be, the bound alone decides.
No kernel may reach another device: no remote copies, remote signals or barrier semaphores. Data moves between devices by JAX's collectives and lax.ppermute only.
A program may use at most 64 MiB of HBM per device.

v0:
```python
import functools
import math

import jax
import jax.numpy as jnp
import ml_dtypes
import numpy as np
from jax import lax
from jax.experimental import pallas as pl
from jax.experimental.pallas import tpu as pltpu
from jax.sharding import PartitionSpec as P

LANES = 128
AXES = ("zc", "zl")


def split_const(table):
    head = table.astype(ml_dtypes.bfloat16)
    tail = (table - head.astype(np.float64)).astype(ml_dtypes.bfloat16)
    return head, tail


@functools.cache
def tables(devices, span):
    length = devices * span
    half = devices // 2
    d = np.arange(devices)
    k = np.arange(half)
    turn = 2.0 * math.pi * (k[:, None] * d[None, :] % devices) / devices
    forward = np.concatenate([np.cos(turn), -np.sin(turn)], axis=0)
    forward[half] = 1.0 - 2.0 * (d % 2)
    weight = np.full(devices, 2.0)
    weight[0] = weight[half] = 1.0
    backward = forward.T * (2.0 * weight / devices)[None, :]
    j = np.arange(span)
    kept = length // 8
    count = 2 * kept // devices
    lag = j[:, None] - j[None, :]
    below = np.where(lag == 0, 1.0, span * np.sin(math.pi * lag / span))
    inner = np.where(lag == 0, count / span, np.sin(math.pi * count * lag / span) / below)
    inner_zero = np.where(lag == 0, (count + 1) / span, np.sin(math.pi * (count + 1) * lag / span) / below)
    twice = LANES // span
    inner = np.kron(np.eye(twice), inner)
    extra = np.kron(np.eye(twice), inner_zero) - inner
    angle = 2.0 * math.pi * (k - half)[:, None] * j[None, :] / length
    cos, sin = np.cos(angle), np.sin(angle)
    cos[0], sin[0] = 1.0, 0.0
    cos = np.tile(cos, (1, twice)).astype(np.float32)
    sin = np.tile(sin, (1, twice)).astype(np.float32)
    return (*split_const(forward), *split_const(inner), *split_const(extra), *split_const(backward), cos, sin)


def halves(values):
    head = values.astype(jnp.bfloat16)
    return head, (values - head.astype(jnp.float32)).astype(jnp.bfloat16)


def dot(a, b):
    return jnp.dot(a, b, preferred_element_type=jnp.float32)


def pack_kernel(v_ref, out_ref, first_ref, last_ref):
    comps, span, merged = v_ref.shape
    pairs = merged // (2 * LANES)
    for c in range(comps):
        for q in range(pairs):
            at = q * 2 * LANES
            both = jnp.concatenate([v_ref[c, :, at : at + LANES], v_ref[c, :, at + LANES : at + 2 * LANES]], axis=0)
            out_ref[pl.ds(c * pairs + q, LANES, stride=comps * pairs), :] = both.T
        first_ref[c : c + 1, :] = v_ref[c, 0:1, :]
        last_ref[c : c + 1, :] = v_ref[c, span - 1 : span, :]


def smooth_kernel(
    x_ref, fh_ref, fl_ref, rh_ref, rl_ref, eh_ref, el_ref, bh_ref, bl_ref, cos_ref, sin_ref, out_ref, z_ref, w_ref
):
    devices = fh_ref.shape[0]
    half = devices // 2
    groups = x_ref.shape[0] // devices
    cos, sin = cos_ref[...], sin_ref[...]
    fh, fl = fh_ref[...], fl_ref[...]
    rh, rl = rh_ref[...], rl_ref[...]
    bh, bl = bh_ref[...], bl_ref[...]
    zeros = []
    for p in range(groups):
        xh, xl = halves(x_ref[pl.ds(p, devices, stride=groups), :])
        y = dot(fh, xh) + dot(fh, xl) + dot(fl, xh)
        re, im = y[:half], y[half:]
        zeros.append(re[0:1])
        z_ref[p, :half] = re * cos + im * sin
        z_ref[p, half:] = im * cos - re * sin
    pad = -groups % 8
    zero_h, zero_l = halves(jnp.concatenate(zeros + [jnp.zeros((pad, LANES), jnp.float32)], axis=0))
    extra = dot(zero_h, eh_ref[...]) + dot(zero_l, eh_ref[...]) + dot(zero_h, el_ref[...])
    for p in range(groups):
        zh, zl = halves(z_ref[p])
        w = dot(zh, rh) + dot(zl, rh) + dot(zh, rl)
        re, im = w[:half], w[half:]
        w_ref[p, :half] = re * cos - im * sin
        w_ref[p, half:] = im * cos + re * sin
        w_ref[p, 0:1] = w_ref[p, 0:1] + extra[p : p + 1]
    for p in range(groups):
        wh, wl = halves(w_ref[p])
        out_ref[pl.ds(p, devices, stride=groups), :] = dot(bh, wh) + dot(bh, wl) + dot(bl, wh)


def forcing_kernel(v_ref, before_ref, after_ref, flow_ref, slope_ref, mask_ref, place_ref, out_ref, *, normal):
    comps, span, merged = v_ref.shape
    lane = lax.broadcasted_iota(jnp.int32, (1, merged), 1)
    row = lax.rem(lane, normal)
    not_top = (row < normal - 1).astype(jnp.float32)
    not_bottom = (row > 0).astype(jnp.float32)
    solid_rows = (1 - mask_ref[...]).astype(jnp.float32)
    solid = lax.dot_general(
        solid_rows.astype(jnp.bfloat16),
        place_ref[...],
        (((0,), (0,)), ((), ())),
        preferred_element_type=jnp.float32,
    )
    flow = -0.25 * flow_ref[...]
    slope = 0.25 * slope_ref[...]
    for c in range(comps):
        v = v_ref[c]
        ahead = pltpu.roll(v, merged - normal, 1)
        behind = pltpu.roll(v, normal, 1)
        upper = pltpu.roll(v, merged - 1, 1) * not_top
        lower = pltpu.roll(v, 1, 1) * not_bottom
        total = flow * (ahead - behind) + 0.05 * (ahead + behind + upper + lower - 4.0 * v)
        if c == 0:
            total = total - slope * v_ref[1]
        plus = jnp.concatenate([v[1:], after_ref[c : c + 1, :]], axis=0)
        minus = jnp.concatenate([before_ref[c : c + 1, :], v[:-1]], axis=0)
        total = total + solid * (0.15 * (plus + minus - 2.0 * v) - 0.4 * v)
        out_ref[c] = total - v


def unpack_kernel(s_ref, f_ref, out_ref):
    comps, span, merged = f_ref.shape
    pairs = merged // (2 * LANES)
    for c in range(comps):
        for q in range(pairs):
            both = s_ref[pl.ds(c * pairs + q, LANES, stride=comps * pairs), :].T
            lo = slice(q * 2 * LANES, q * 2 * LANES + LANES)
            hi = slice(q * 2 * LANES + LANES, (q + 1) * 2 * LANES)
            out_ref[c, :, lo] = f_ref[c, :, lo] + both[:span]
            out_ref[c, :, hi] = f_ref[c, :, hi] + both[span:]


def exchange(rows, devices):
    spread = lax.all_to_all(rows.reshape(devices, 1, -1), AXES, split_axis=0, concat_axis=0, tiled=True)
    return spread.reshape(rows.shape)


def body(velocity, base_flow, slot_mask):
    span, comps, merged = velocity.shape
    normal = base_flow.shape[0]
    planes = merged // normal
    wall_rows = slot_mask.shape[0]
    devices = lax.axis_size(AXES)
    groups = comps * merged // devices // (LANES // span)
    f32 = jnp.float32
    v = jnp.transpose(velocity, (1, 0, 2))
    edge = jax.ShapeDtypeStruct((comps, merged), f32)
    rows = jax.ShapeDtypeStruct((devices * groups, LANES), f32)
    sent, first, last = pl.pallas_call(pack_kernel, out_shape=(rows, edge, edge))(v)
    got = exchange(sent, devices)
    before = lax.ppermute(last, AXES, [(i, (i + 1) % devices) for i in range(devices)])
    after = lax.ppermute(first, AXES, [((i + 1) % devices, i) for i in range(devices)])
    padded = jnp.pad(base_flow, 1)
    flow = jnp.tile(base_flow, planes)[None]
    slope = jnp.tile(padded[2:] - padded[:-2], planes)[None]
    lane = np.arange(merged) % normal
    place = jnp.asarray((lane[None, :] == np.arange(wall_rows)[:, None]).astype(ml_dtypes.bfloat16))
    forcing = pl.pallas_call(
        functools.partial(forcing_kernel, normal=normal),
        out_shape=jax.ShapeDtypeStruct(v.shape, f32),
        cost_estimate=pl.CostEstimate(flops=30 * v.size, bytes_accessed=8 * v.size, transcendentals=0),
    )(v, before, after, flow, slope, slot_mask, place)
    smoothed = pl.pallas_call(
        smooth_kernel,
        out_shape=rows,
        scratch_shapes=[pltpu.VMEM((groups, devices, LANES), f32)] * 2,
    )(got, *(jnp.asarray(t) for t in tables(devices, span)))
    back = exchange(smoothed, devices)
    out = pl.pallas_call(unpack_kernel, out_shape=jax.ShapeDtypeStruct(v.shape, f32))(back, forcing)
    return jnp.transpose(out, (1, 0, 2))


def solution(mesh):
    in_specs = (P(AXES, None, None), P(), P(None, AXES))
    out_specs = P(AXES, None, None)
    return jax.shard_map(body, mesh=mesh, in_specs=in_specs, out_specs=out_specs, check_vma=False)
```

profile of v0, /device:TPU:0, one launch (start us, length us, event | category | flops | bytes accessed | tf_op | source)
XLA Modules:
  0.0 72.5 jit_solution(8503555384533227997)
XLA Ops:
  0.0 2.7 %shard_map.136 = (f32[2304,128]{1,0:T(8,128)}, f32[3,1536]{1,0:T(4,128)}, f32[3,1536]{1,0:T(4,128)}) custom-call(f32[3,64,1536]{2,1,0:T(8,128)} %bitcast.7), custom_call_target="tpu_custom_call" | custom-call | tf_op jit(solution)/shard_map/pallas_call | solution.py:165
  2.7 31.8 %all_to_all.10 = f32[128,1,2304]{2,1,0:T(1,128)} all-to-all(f32[128,1,2304]{2,1,0:T(1,128)} %bitcast.11), channel_id=1, replica_groups=mesh['zc'=16,'zl'=8] {'zc','zl'}, dimensions={0} | all-to-all | bytes 2359296 | tf_op jit(solution)/shard_map/all_to_all | solution.py:150
  34.5 4.1 %shard_map.137 = f32[2304,128]{1,0:T(8,128)} custom-call(f32[2304,128]{1,0:T(8,128)} %bitcast.10, bf16[128,128]{1,0:T(8,128)(2,1)} %constant.26.clone.fh_ref, bf16[128,128]{1,0:T(8,128)(2,1)} %constant.27.clone.fl_ref, bf16[128,128]{1,0:T(8,128)(2,1)} %constant.28.clone.rh_ref, bf16[128,128]{1,0:T(8,128)(2,1)} %constant.29.clone.rl_ref, ...), custom_call_target="tpu_custom_call" | custom-call | tf_op jit(solution)/shard_map/pallas_call | solution.py:179
  38.6 0.0 copy-start.5
  38.6 0.0 copy-start.4
  38.6 0.0 copy-start.3
  38.6 4.8 %all-to-all-start.1 = ((f32[128,1,2304]{2,1,0:T(1,128)}), f32[128,1,2304]{2,1,0:T(1,128)S(1)}, u32[]{:S(2)}, u32[]{:S(2)}) async-start(f32[128,1,2304]{2,1,0:T(1,128)} %bitcast.9), calls=%async_computation.1 | async-start | bytes 2359296 | tf_op jit(solution)/shard_map/all_to_all | solution.py:150
  43.4 0.0 copy-done.5
  43.4 0.1 collective-permute-start
  43.5 0.0 copy-done.4
  43.5 7.2 %collective-permute-start.1 = (f32[3,1536]{1,0:T(4,128)S(1)}, f32[3,1536]{1,0:T(4,128)S(1)}, u32[]{:S(2)}, u32[]{:S(2)}) collective-permute-start(f32[3,1536]{1,0:T(4,128)S(1)} %copy-done.4), channel_id=1, source_target_pairs={{1,0},{2,1},{3,2},{4,3},{5,4},{6,5},{7,6},{8,7},{9,8},{10,9},{11,1... | collective-permute-start | bytes 55304 | tf_op jit(solution)/shard_map/ppermute | solution.py:168
  50.7 0.0 copy-done.3
  50.7 0.1 slice_subtract_fusion
  50.7 0.7 broadcast_in_dim_tile.7.slope_ref
  51.4 0.7 broadcast_in_dim_tile.6.flow_ref
  52.1 11.3 %collective-permute-done.before_ref = f32[3,1536]{1,0:T(4,128)S(1)} collective-permute-done((f32[3,1536]{1,0:T(4,128)S(1)}, f32[3,1536]{1,0:T(4,128)S(1)}, u32[]{:S(2)}, u32[]{:S(2)}) %collective-permute-start) | collective-permute-done | bytes 18464 | tf_op jit(solution)/shard_map/ppermute | solution.py:167
  63.4 0.0 copy-start.1
  63.4 0.0 collective-permute-done.1.after_ref
  63.4 0.6 copy-done.1
  64.0 0.0 copy-start.2
  64.0 0.6 copy-done.2
  64.6 3.8 %shard_map.138.f_ref = f32[3,64,1536]{2,1,0:T(8,128)} custom-call(f32[3,64,1536]{2,1,0:T(8,128)} %bitcast.8, f32[3,1536]{1,0:T(4,128)} %copy-done.1, f32[3,1536]{1,0:T(4,128)} %copy-done.2, f32[1,1536]{1,0:T(1,128)} %broadcast_in_dim_tile.6.flow_ref, f32[1,1536]{1,0:T(1,128)} %broadcast_in_dim_tile.7.slope_ref, s32[8,64]{1,0:T(8,128)} %mask_ref.1, ...), custom_call_target="tpu_custom_call" | custom-call | flops 8847360 | bytes 2359296 | tf_op jit(solution)/shard_map/pallas_call | solution.py:174
  68.4 0.0 all-to-all-done.1
  68.4 0.0 copy-start
  68.4 1.0 %copy-done = f32[128,1,2304]{2,1,0:T(1,128)} copy-done((f32[128,1,2304]{2,1,0:T(1,128)}, f32[128,1,2304]{2,1,0:T(1,128)S(1)}, u32[]{:S(2)}) %copy-start) | copy-done | bytes 1179672
  69.5 3.0 %shard_map.139 = f32[3,64,1536]{2,1,0:T(8,128)} custom-call(f32[2304,128]{1,0:T(8,128)} %bitcast.6, f32[3,64,1536]{2,1,0:T(8,128)} %shard_map.138.f_ref), custom_call_target="tpu_custom_call" | custom-call | tf_op jit(solution)/shard_map/pallas_call | solution.py:185
  (2 shorter events, 0.0 us)
Async XLA Ops:
  38.6 4.8 %copy-start.5 = (f32[3,1536]{1,0:T(4,128)S(1)}, f32[3,1536]{1,0:T(4,128)}, u32[]{:S(2)}) copy-start(f32[3,1536]{1,0:T(4,128)} %get-tuple-element.9) | copy-start | bytes 55300
  38.6 4.9 %copy-start.4 = (f32[3,1536]{1,0:T(4,128)S(1)}, f32[3,1536]{1,0:T(4,128)}, u32[]{:S(2)}) copy-start(f32[3,1536]{1,0:T(4,128)} %get-tuple-element.10) | copy-start | bytes 55300
  38.6 12.1 %copy-start.3 = (f32[192]{0:T(256)S(1)}, f32[192]{0:T(256)}, u32[]{:S(2)}) copy-start(f32[192]{0:T(256)} %param.15) | copy-start | bytes 2308
  38.6 29.8 %all-to-all-start.1 = ((f32[128,1,2304]{2,1,0:T(1,128)}), f32[128,1,2304]{2,1,0:T(1,128)S(1)}, u32[]{:S(2)}, u32[]{:S(2)}) async-start(f32[128,1,2304]{2,1,0:T(1,128)} %bitcast.9), calls=%async_computation.1 | async-start | bytes 2359296 | tf_op jit(solution)/shard_map/all_to_all | solution.py:150
  43.4 20.0 %collective-permute-start = (f32[3,1536]{1,0:T(4,128)S(1)}, f32[3,1536]{1,0:T(4,128)S(1)}, u32[]{:S(2)}, u32[]{:S(2)}) collective-permute-start(f32[3,1536]{1,0:T(4,128)S(1)} %copy-done.5), channel_id=1, source_target_pairs={{0,1},{1,2},{2,3},{3,4},{4,5},{5,6},{6,7},{7,8},{8,9},{9,10},{10,1... | collective-permute-start | bytes 55304 | tf_op jit(solution)/shard_map/ppermute | solution.py:167
  43.5 19.9 %collective-permute-start.1 = (f32[3,1536]{1,0:T(4,128)S(1)}, f32[3,1536]{1,0:T(4,128)S(1)}, u32[]{:S(2)}, u32[]{:S(2)}) collective-permute-start(f32[3,1536]{1,0:T(4,128)S(1)} %copy-done.4), channel_id=1, source_target_pairs={{1,0},{2,1},{3,2},{4,3},{5,4},{6,5},{7,6},{8,7},{9,8},{10,9},{11,1... | collective-permute-start | bytes 55304 | tf_op jit(solution)/shard_map/ppermute | solution.py:168
  63.4 0.6 copy-start.1
  64.0 0.6 copy-start.2
  68.4 1.0 %copy-start = (f32[128,1,2304]{2,1,0:T(1,128)}, f32[128,1,2304]{2,1,0:T(1,128)S(1)}, u32[]{:S(2)}) copy-start(f32[128,1,2304]{2,1,0:T(1,128)S(1)} %all-to-all-done.1) | copy-start | bytes 3538948
where the time goes:
time: 72.9 us; the launch traced here: 72.5 us
  blocking collectives  31.8 us (44%)
  Pallas kernels  13.6 us (19%)
  starting transfers between devices  12 us (16%)
  waiting for transfers between devices  11.3 us (16%)
  local copies, waits for them, and re-layouts  3.62 us (5%)
    all_to_all x1, blocking collectives, exchange(): lax.all_to_all(rows.reshape(devices, 1, -1), AXES, split_axis=0, concat_a...  31.8 us
    ppermute x1, waiting for transfers between devices, body(): lax.ppermute(last, AXES, [(i, (i + 1) % devices) for i in range(devices)])  11.3 us
    ppermute x1, starting transfers between devices, body(): lax.ppermute(first, AXES, [((i + 1) % devices, i) for i in range(devices)])  7.15 us
    all_to_all x1, starting transfers between devices, exchange(): lax.all_to_all(rows.reshape(devices, 1, -1), AXES, split_axis=0, concat_a...  4.78 us
    pallas_call x1, Pallas kernels, body(): pl.pallas_call(smooth_kernel, out_shape=rows, scratch_shapes=[pltpu.VMEM(...  4.13 us
    pallas_call x1, Pallas kernels, body(): pl.pallas_call(functools.partial(forcing_kernel, normal=normal), out_shap...  3.82 us
    pallas_call x1, Pallas kernels, body(): pl.pallas_call(unpack_kernel, out_shape=jax.ShapeDtypeStruct(v.shape, f32))  3.01 us
    pallas_call x1, Pallas kernels, body(): pl.pallas_call(pack_kernel, out_shape=(rows, edge, edge))(v)  2.65 us
  transfers between devices with their start and end apart: 3, of which 1 were waited for; matrix products, arithmetic and copies ran while one was open for 2% of the time, Pallas kernels for 5%

commit v1 on v0

v1 whole, which is shorter than its diff:
```python
import functools
import math

import jax
import jax.numpy as jnp
import ml_dtypes
import numpy as np
from jax import lax
from jax.experimental import pallas as pl
from jax.experimental.pallas import tpu as pltpu
from jax.sharding import PartitionSpec as P

LANES = 128
AXES = ("zc", "zl")


def split_const(table):
    head = table.astype(ml_dtypes.bfloat16)
    tail = (table - head.astype(np.float64)).astype(ml_dtypes.bfloat16)
    return head, tail


@functools.cache
def tables(devices, span):
    length = devices * span
    half = devices // 2
    d = np.arange(devices)
    k = np.arange(half)
    turn = 2.0 * math.pi * (k[:, None] * d[None, :] % devices) / devices
    forward = np.concatenate([np.cos(turn), -np.sin(turn)], axis=0)
    forward[half] = 1.0 - 2.0 * (d % 2)
    weight = np.full(devices, 2.0)
    weight[0] = weight[half] = 1.0
    backward = forward.T * (2.0 * weight / devices)[None, :]
    j = np.arange(span)
    kept = length // 8
    count = 2 * kept // devices
    lag = j[:, None] - j[None, :]
    below = np.where(lag == 0, 1.0, span * np.sin(math.pi * lag / span))
    inner = np.where(lag == 0, count / span, np.sin(math.pi * count * lag / span) / below)
    inner_zero = np.where(lag == 0, (count + 1) / span, np.sin(math.pi * (count + 1) * lag / span) / below)
    twice = LANES // span
    inner = np.kron(np.eye(twice), inner)
    extra = np.kron(np.eye(twice), inner_zero) - inner
    angle = 2.0 * math.pi * (k - half)[:, None] * j[None, :] / length
    cos, sin = np.cos(angle), np.sin(angle)
    cos[0], sin[0] = 1.0, 0.0
    cos = np.tile(cos, (1, twice)).astype(np.float32)
    sin = np.tile(sin, (1, twice)).astype(np.float32)
    return (both_rows(forward), both_lanes(inner), both_lanes(extra), both_rows(backward), cos, sin)


def both_rows(table):
    head, tail = split_const(table)
    return np.block([[head, head], [tail, tail]])


def both_lanes(table):
    head, tail = split_const(table)
    return np.block([[head, tail], [head, tail]])


def halves(values, axis):
    head = values.astype(jnp.bfloat16)
    tail = (values - head.astype(jnp.float32)).astype(jnp.bfloat16)
    return jnp.concatenate([head, tail], axis=axis)


def dot_rows(table, values):
    both = jnp.dot(table, halves(values, 0), preferred_element_type=jnp.float32)
    rows = table.shape[0] // 2
    return both[:rows] + both[rows:]


def dot_lanes(values, table):
    both = jnp.dot(halves(values, 1), table, preferred_element_type=jnp.float32)
    lanes = table.shape[1] // 2
    return both[:, :lanes] + both[:, lanes:]


def pack_kernel(v_ref, out_ref, first_ref, last_ref):
    _, span, merged = v_ref.shape
    c = pl.program_id(0)
    pairs = merged // (2 * LANES)
    groups = out_ref.shape[0] // LANES
    for q in range(pairs):
        at = q * 2 * LANES
        both = jnp.concatenate([v_ref[0, :, at : at + LANES], v_ref[0, :, at + LANES : at + 2 * LANES]], axis=0)
        out_ref[pl.ds(c * pairs + q, LANES, stride=groups), :] = both.T
    first_ref[pl.ds(c, 1), :] = v_ref[0, 0:1, :]
    last_ref[pl.ds(c, 1), :] = v_ref[0, span - 1 : span, :]


def smooth_kernel(x_ref, f_ref, r_ref, e_ref, b_ref, cos_ref, sin_ref, out_ref):
    devices = f_ref.shape[0] // 2
    half = devices // 2
    groups = x_ref.shape[0] // devices
    cos, sin = cos_ref[...], sin_ref[...]
    forward, inner, backward = f_ref[...], r_ref[...], b_ref[...]
    for p in range(0, groups, 2):
        pair = [x_ref[pl.ds(p + i, devices, stride=groups), :] for i in range(2)]
        y = dot_rows(forward, jnp.concatenate(pair, axis=1))
        turned = []
        for i in range(2):
            re = y[:half, i * LANES : (i + 1) * LANES]
            im = y[half:, i * LANES : (i + 1) * LANES]
            turned += [re * cos + im * sin, im * cos - re * sin]
        w = dot_lanes(jnp.concatenate(turned, axis=0), inner)
        lone = dot_lanes(jnp.concatenate([y[0:8, :LANES], y[0:8, LANES:]], axis=0), e_ref[...])
        back = []
        for i in range(2):
            re = w[i * devices : i * devices + half]
            im = w[i * devices + half : (i + 1) * devices]
            first = lax.broadcasted_iota(jnp.int32, (8, LANES), 0) == 0
            top = re * cos - im * sin
            top = jnp.concatenate([top[:8] + jnp.where(first, lone[i * 8 : (i + 1) * 8], 0.0), top[8:]], axis=0)
            back.append(jnp.concatenate([top, im * cos + re * sin], axis=0))
        y = dot_rows(backward, jnp.concatenate(back, axis=1))
        for i in range(2):
            out_ref[pl.ds(p + i, devices, stride=groups), :] = y[:, i * LANES : (i + 1) * LANES]


def forcing_kernel(v_ref, before_ref, after_ref, flow_ref, slope_ref, mask_ref, place_ref, out_ref, *, normal):
    comps, span, merged = v_ref.shape
    lane = lax.broadcasted_iota(jnp.int32, (1, merged), 1)
    row = lax.rem(lane, normal)
    not_top = (row < normal - 1).astype(jnp.float32)
    not_bottom = (row > 0).astype(jnp.float32)
    solid_rows = (1 - mask_ref[...]).astype(jnp.float32)
    solid = lax.dot_general(
        solid_rows.astype(jnp.bfloat16),
        place_ref[...],
        (((0,), (0,)), ((), ())),
        preferred_element_type=jnp.float32,
    )
    flow = -0.25 * flow_ref[...]
    slope = 0.25 * slope_ref[...]
    for c in range(comps):
        v = v_ref[c]
        ahead = pltpu.roll(v, merged - normal, 1)
        behind = pltpu.roll(v, normal, 1)
        upper = pltpu.roll(v, merged - 1, 1) * not_top
        lower = pltpu.roll(v, 1, 1) * not_bottom
        total = flow * (ahead - behind) + 0.05 * (ahead + behind + upper + lower - 4.0 * v)
        if c == 0:
            total = total - slope * v_ref[1]
        plus = jnp.concatenate([v[1:], after_ref[c : c + 1, :]], axis=0)
        minus = jnp.concatenate([before_ref[c : c + 1, :], v[:-1]], axis=0)
        total = total + solid * (0.15 * (plus + minus - 2.0 * v) - 0.4 * v)
        out_ref[c] = total - v


def unpack_kernel(s_ref, f_ref, out_ref):
    _, span, merged = out_ref.shape
    c = pl.program_id(0)
    pairs = merged // (2 * LANES)
    groups = s_ref.shape[0] // LANES
    for q in range(pairs):
        both = s_ref[pl.ds(c * pairs + q, LANES, stride=groups), :].T
        lo = slice(q * 2 * LANES, q * 2 * LANES + LANES)
        hi = slice(q * 2 * LANES + LANES, (q + 1) * 2 * LANES)
        out_ref[0, :, lo] = f_ref[c, :, lo] + both[:span]
        out_ref[0, :, hi] = f_ref[c, :, hi] + both[span:]


def exchange(rows, devices):
    spread = lax.all_to_all(rows.reshape(devices, 1, -1), AXES, split_axis=0, concat_axis=0, tiled=True)
    return spread.reshape(rows.shape)


def in_vmem(array):
    return pltpu.with_memory_space_constraint(array, pltpu.VMEM)


def body(velocity, base_flow, slot_mask):
    span, comps, merged = velocity.shape
    normal = base_flow.shape[0]
    planes = merged // normal
    wall_rows = slot_mask.shape[0]
    devices = lax.axis_size(AXES)
    groups = comps * merged // devices // (LANES // span)
    f32 = jnp.float32
    here = pl.BlockSpec(memory_space=pltpu.VMEM)
    part = pl.BlockSpec((1, span, merged), lambda c: (c, 0, 0))
    edge = pltpu.VMEM((comps, merged), f32)
    rows = pltpu.VMEM((devices * groups, LANES), f32)
    v = jnp.transpose(velocity, (1, 0, 2))
    sent, first, last = pl.pallas_call(
        pack_kernel, grid=(comps,), in_specs=[part], out_specs=(here,) * 3, out_shape=(rows, edge, edge)
    )(v)
    got = exchange(sent, devices)
    before = lax.ppermute(last, AXES, [(i, (i + 1) % devices) for i in range(devices)])
    after = lax.ppermute(first, AXES, [((i + 1) % devices, i) for i in range(devices)])
    got, before, after = lax.optimization_barrier((got, before, after))
    smoothed = pl.pallas_call(
        smooth_kernel,
        in_specs=[here] * 7,
        out_specs=here,
        out_shape=rows,
        cost_estimate=pl.CostEstimate(flops=0, bytes_accessed=10_000_000, transcendentals=0),
    )(in_vmem(got), *(in_vmem(jnp.asarray(t)) for t in tables(devices, span)))
    back = exchange(smoothed, devices)
    padded = jnp.pad(base_flow, 1)
    flow = jnp.tile(base_flow, planes)[None]
    slope = jnp.tile(padded[2:] - padded[:-2], planes)[None]
    lane = np.arange(merged) % normal
    place = jnp.asarray((lane[None, :] == np.arange(wall_rows)[:, None]).astype(ml_dtypes.bfloat16))
    forcing = pl.pallas_call(
        functools.partial(forcing_kernel, normal=normal),
        in_specs=[here] * 7,
        out_specs=here,
        out_shape=pltpu.VMEM(v.shape, f32),
        cost_estimate=pl.CostEstimate(flops=0, bytes_accessed=10_000_000, transcendentals=0),
    )(v, in_vmem(before), in_vmem(after), flow, slope, slot_mask, place)
    out = pl.pallas_call(
        unpack_kernel,
        grid=(comps,),
        in_specs=[here] * 2,
        out_specs=part,
        out_shape=jax.ShapeDtypeStruct(v.shape, f32),
    )(in_vmem(back), in_vmem(forcing))
    return jnp.transpose(out, (1, 0, 2))


def solution(mesh):
    in_specs = (P(AXES, None, None), P(), P(None, AXES))
    out_specs = P(AXES, None, None)
    return jax.shard_map(body, mesh=mesh, in_specs=in_specs, out_specs=out_specs, check_vma=False)
```

time: 72.9 us -> 67.3 us (0.923)
  blocking collectives: 31.8 us -> 0 us
  waiting for transfers between devices: 11.3 us -> 29.9 us
  starting transfers between devices: 12 us -> 23.1 us
  local copies, waits for them, and re-layouts: 3.62 us -> 1.39 us
  Pallas kernels: 13.6 us -> 11.9 us
    all_to_all x1 -> x0, blocking collectives: 31.8 us -> none  [exchange(): lax.all_to_all(rows.reshape(devices, 1, -1), AXES, split_axis=0, concat_a...]
    all_to_all x1 -> x2, waiting for transfers between devices: 0.01 us -> 17.1 us  [exchange(): lax.all_to_all(rows.reshape(devices, 1, -1), AXES, split_axis=0, concat_a...]
    all_to_all x1 -> x2, starting transfers between devices: 4.78 us -> 15.9 us  [exchange(): lax.all_to_all(rows.reshape(devices, 1, -1), AXES, split_axis=0, concat_a...]
    unnamed x12 -> x14, local copies, waits for them, and re-layouts: 2.26 us -> 0.03 us
    pallas_call x4, Pallas kernels: 13.6 us -> 11.9 us  [the longest x1 3.9 us: body(): pl.pallas_call(smooth_kernel, in_specs=[here] * 7, out_specs=here, out_sh...]
    ppermute x1, waiting for transfers between devices: 11.3 us -> 12.8 us  [body(): lax.ppermute(last, AXES, [(i, (i + 1) % devices) for i in range(devices)])]
  transfers between devices with their start and end apart: 3 -> 4, of which waited for: 1 -> 3; matrix products, arithmetic and copies ran while one was open for 2% -> 2% of each run, Pallas kernels for 5% -> 4%
where the time goes in v1:
time: 67.3 us; the launch traced here: 66.5 us
  waiting for transfers between devices  29.9 us (44%)
  starting transfers between devices  23.1 us (34%)
  Pallas kernels  11.9 us (18%)
  local copies, waits for them, and re-layouts  1.39 us (2%)
    all_to_all x2, waiting for transfers between devices, exchange(): lax.all_to_all(rows.reshape(devices, 1, -1), AXES, split_axis=0, concat_a...  17.1 us
    all_to_all x2, starting transfers between devices, exchange(): lax.all_to_all(rows.reshape(devices, 1, -1), AXES, split_axis=0, concat_a...  15.9 us
    ppermute x1, waiting for transfers between devices, body(): lax.ppermute(last, AXES, [(i, (i + 1) % devices) for i in range(devices)])  12.8 us
    ppermute x1, starting transfers between devices, body(): lax.ppermute(first, AXES, [((i + 1) % devices, i) for i in range(devices)])  7.16 us
    pallas_call x1, Pallas kernels, body(): pl.pallas_call(smooth_kernel, in_specs=[here] * 7, out_specs=here, out_sh...  3.9 us
    pallas_call x1, Pallas kernels, body(): pl.pallas_call(pack_kernel, grid=(comps,), in_specs=[part], out_specs=(he...  3.34 us
    pallas_call x1, Pallas kernels, body(): pl.pallas_call(functools.partial(forcing_kernel, normal=normal), in_specs...  2.79 us
    pallas_call x1, Pallas kernels, body(): pl.pallas_call(unpack_kernel, grid=(comps,), in_specs=[here] * 2, out_spe...  1.83 us
  transfers between devices with their start and end apart: 4, of which 3 were waited for; matrix products, arithmetic and copies ran while one was open for 2% of the time, Pallas kernels for 4%

profile of v1, /device:TPU:0, one launch (start us, length us, event | category | flops | bytes accessed | tf_op | source)
XLA Modules:
  0.0 66.5 jit_solution(1898340646398744514)
XLA Ops:
  0.0 3.3 %shard_map.100 = (f32[2304,128]{1,0:T(8,128)}, f32[3,1536]{1,0:T(4,128)S(1)}, f32[3,1536]{1,0:T(4,128)S(1)}) custom-call(f32[3,64,1536]{2,1,0:T(8,128)} %bitcast.8), custom_call_target="tpu_custom_call" | custom-call | tf_op jit(solution)/shard_map/pallas_call | solution.py:188
  3.3 0.0 copy-start
  3.3 0.0 copy-start.1
  3.4 0.0 copy-start.2
  3.4 0.0 copy-start.3
  3.4 0.0 copy-start.4
  3.4 0.0 copy-start.5
  3.4 11.1 %all-to-all-start = ((f32[128,1,2304]{2,1,0:T(1,128)}), f32[128,1,2304]{2,1,0:T(1,128)S(1)}, u32[]{:S(2)}, u32[]{:S(2)}) async-start(f32[128,1,2304]{2,1,0:T(1,128)} %bitcast.1), calls=%async_computation | async-start | bytes 2359296 | tf_op jit(solution)/shard_map/all_to_all | solution.py:167
  14.5 0.1 collective-permute-start
  14.6 7.2 %collective-permute-start.1 = (f32[3,1536]{1,0:T(4,128)S(1)}, f32[3,1536]{1,0:T(4,128)S(1)}, u32[]{:S(2)}, u32[]{:S(2)}) collective-permute-start(f32[3,1536]{1,0:T(4,128)S(1)} %get-tuple-element.13), channel_id=1, source_target_pairs={{1,0},{2,1},{3,2},{4,3},{5,4},{6,5},{7,6},{8,7},{9,8},{10,9},{11,1... | collective-permute-start | bytes 55304 | tf_op jit(solution)/shard_map/ppermute | solution.py:193
  21.8 12.8 %collective-permute-done.before_ref = f32[3,1536]{1,0:T(4,128)S(1)} collective-permute-done((f32[3,1536]{1,0:T(4,128)S(1)}, f32[3,1536]{1,0:T(4,128)S(1)}, u32[]{:S(2)}, u32[]{:S(2)}) %collective-permute-start) | collective-permute-done | bytes 18464 | tf_op jit(solution)/shard_map/ppermute | solution.py:192
  34.5 0.0 collective-permute-done.1.after_ref
  34.5 0.8 %all-to-all-done = f32[128,1,2304]{2,1,0:T(1,128)S(1)} async-done(((f32[128,1,2304]{2,1,0:T(1,128)}), f32[128,1,2304]{2,1,0:T(1,128)S(1)}, u32[]{:S(2)}, u32[]{:S(2)}) %all-to-all-start) | async-done | bytes 1179680 | tf_op jit(solution)/shard_map/all_to_all | solution.py:167
  35.4 0.0 copy-done
  35.4 0.0 copy-done.1
  35.4 0.0 copy-done.2
  35.4 0.0 copy-done.3
  35.4 0.0 copy-done.4
  35.4 0.0 copy-done.5
  35.4 3.9 %shard_map.101 = f32[2304,128]{1,0:T(8,128)} custom-call(f32[2304,128]{1,0:T(8,128)S(1)} %bitcast.7, bf16[256,256]{1,0:T(8,128)(2,1)S(1)} %copy-done.3, bf16[256,256]{1,0:T(8,128)(2,1)S(1)} %copy-done.2, bf16[256,256]{1,0:T(8,128)(2,1)S(1)} %copy-done.1, bf16[256,256]{1,0:T(8,128)(2,1)S(1)} %copy-done, f32[64,128]{1,0:T(8,128)S(1)} %copy-done.5, ...), custom_call_target="tpu_custom_call" | custom-call | bytes 10000000 | tf_op jit(solution)/shard_map/pallas_call | solution.py:195
  39.3 0.0 copy-start.6
  39.3 4.8 %all-to-all-start.1 = ((f32[128,1,2304]{2,1,0:T(1,128)}), f32[128,1,2304]{2,1,0:T(1,128)S(1)}, u32[]{:S(2)}, u32[]{:S(2)}) async-start(f32[128,1,2304]{2,1,0:T(1,128)} %bitcast.3), calls=%async_computation.1 | async-start | bytes 2359296 | tf_op jit(solution)/shard_map/all_to_all | solution.py:167
  44.1 0.0 copy-done.6
  44.1 0.1 slice_subtract_fusion
  44.2 0.7 %broadcast_in_dim_tile.7.slope_ref = f32[1,1536]{1,0:T(1,128)} reshape(f32[8,192]{1,0:T(8,128)S(1)} %tile.5) | data formatting | bytes 12288 | tf_op jit(solution)/shard_map/broadcast_in_dim;tile | solution.py:205
  44.8 0.7 %broadcast_in_dim_tile.6.flow_ref = f32[1,1536]{1,0:T(1,128)} reshape(f32[8,192]{1,0:T(8,128)S(1)} %tile.4) | data formatting | bytes 12288 | tf_op jit(solution)/shard_map/broadcast_in_dim;tile | solution.py:204
  45.5 2.8 %shard_map.102.f_ref = f32[3,64,1536]{2,1,0:T(8,128)S(1)} custom-call(f32[3,64,1536]{2,1,0:T(8,128)} %bitcast.9, f32[3,1536]{1,0:T(4,128)S(1)} %collective-permute-done.before_ref, f32[3,1536]{1,0:T(4,128)S(1)} %collective-permute-done.1.after_ref, f32[1,1536]{1,0:T(1,128)} %broadcast_in_dim_tile.6.flow_ref, f32[1,1536]{1,0:T(1,128)} %broadcast_in_dim_tile.7.slope_ref, ...), custom_call_target="tpu_custom_call" | custom-call | bytes 10000000 | tf_op jit(solution)/shard_map/pallas_call | solution.py:208
  48.3 16.3 %all-to-all-done.1 = f32[128,1,2304]{2,1,0:T(1,128)S(1)} async-done(((f32[128,1,2304]{2,1,0:T(1,128)}), f32[128,1,2304]{2,1,0:T(1,128)S(1)}, u32[]{:S(2)}, u32[]{:S(2)}) %all-to-all-start.1) | async-done | bytes 1179680 | tf_op jit(solution)/shard_map/all_to_all | solution.py:167
  64.6 1.8 %shard_map.103 = f32[3,64,1536]{2,1,0:T(8,128)} custom-call(f32[2304,128]{1,0:T(8,128)S(1)} %bitcast.6, f32[3,64,1536]{2,1,0:T(8,128)S(1)} %shard_map.102.f_ref), custom_call_target="tpu_custom_call" | custom-call | tf_op jit(solution)/shard_map/pallas_call | solution.py:215
  (2 shorter events, 0.0 us)
Async XLA Ops:
  3.3 32.0 %copy-start = (bf16[256,256]{1,0:T(8,128)(2,1)S(1)}, bf16[256,256]{1,0:T(8,128)(2,1)}, u32[]{:S(2)}) copy-start(bf16[256,256]{1,0:T(8,128)(2,1)} %constant.20.clone.b_ref) | copy-start | bytes 393220
  3.3 32.0 %copy-start.1 = (bf16[256,256]{1,0:T(8,128)(2,1)S(1)}, bf16[256,256]{1,0:T(8,128)(2,1)}, u32[]{:S(2)}) copy-start(bf16[256,256]{1,0:T(8,128)(2,1)} %constant.19.clone.e_ref) | copy-start | bytes 393220
  3.4 32.0 %copy-start.2 = (bf16[256,256]{1,0:T(8,128)(2,1)S(1)}, bf16[256,256]{1,0:T(8,128)(2,1)}, u32[]{:S(2)}) copy-start(bf16[256,256]{1,0:T(8,128)(2,1)} %constant.18.clone.r_ref) | copy-start | bytes 393220
  3.4 32.0 %copy-start.3 = (bf16[256,256]{1,0:T(8,128)(2,1)S(1)}, bf16[256,256]{1,0:T(8,128)(2,1)}, u32[]{:S(2)}) copy-start(bf16[256,256]{1,0:T(8,128)(2,1)} %constant.17.clone.f_ref) | copy-start | bytes 393220
  3.4 32.0 %copy-start.4 = (f32[64,128]{1,0:T(8,128)S(1)}, f32[64,128]{1,0:T(8,128)}, u32[]{:S(2)}) copy-start(f32[64,128]{1,0:T(8,128)} %constant.22.clone.sin_ref) | copy-start | bytes 98308
  3.4 32.0 %copy-start.5 = (f32[64,128]{1,0:T(8,128)S(1)}, f32[64,128]{1,0:T(8,128)}, u32[]{:S(2)}) copy-start(f32[64,128]{1,0:T(8,128)} %constant.21.clone.cos_ref) | copy-start | bytes 98308
  3.4 32.0 %all-to-all-start = ((f32[128,1,2304]{2,1,0:T(1,128)}), f32[128,1,2304]{2,1,0:T(1,128)S(1)}, u32[]{:S(2)}, u32[]{:S(2)}) async-start(f32[128,1,2304]{2,1,0:T(1,128)} %bitcast.1), calls=%async_computation | async-start | bytes 2359296 | tf_op jit(solution)/shard_map/all_to_all | solution.py:167
  14.5 20.0 %collective-permute-start = (f32[3,1536]{1,0:T(4,128)S(1)}, f32[3,1536]{1,0:T(4,128)S(1)}, u32[]{:S(2)}, u32[]{:S(2)}) collective-permute-start(f32[3,1536]{1,0:T(4,128)S(1)} %get-tuple-element.12), channel_id=1, source_target_pairs={{0,1},{1,2},{2,3},{3,4},{4,5},{5,6},{6,7},{7,8},{8,9},{9,10},{10,1... | collective-permute-start | bytes 55304 | tf_op jit(solution)/shard_map/ppermute | solution.py:192
  14.6 19.9 %collective-permute-start.1 = (f32[3,1536]{1,0:T(4,128)S(1)}, f32[3,1536]{1,0:T(4,128)S(1)}, u32[]{:S(2)}, u32[]{:S(2)}) collective-permute-start(f32[3,1536]{1,0:T(4,128)S(1)} %get-tuple-element.13), channel_id=1, source_target_pairs={{1,0},{2,1},{3,2},{4,3},{5,4},{6,5},{7,6},{8,7},{9,8},{10,9},{11,1... | collective-permute-start | bytes 55304 | tf_op jit(solution)/shard_map/ppermute | solution.py:193
  39.3 4.8 %copy-start.6 = (f32[192]{0:T(256)S(1)}, f32[192]{0:T(256)}, u32[]{:S(2)}) copy-start(f32[192]{0:T(256)} %param.11) | copy-start | bytes 2308
  39.3 25.3 %all-to-all-start.1 = ((f32[128,1,2304]{2,1,0:T(1,128)}), f32[128,1,2304]{2,1,0:T(1,128)S(1)}, u32[]{:S(2)}, u32[]{:S(2)}) async-start(f32[128,1,2304]{2,1,0:T(1,128)} %bitcast.3), calls=%async_computation.1 | async-start | bytes 2359296 | tf_op jit(solution)/shard_map/all_to_all | solution.py:167

commit v2 on v1

--- a/solution.py
+++ b/solution.py
@@ -78,49 +78,79 @@
     return both[:, :lanes] + both[:, lanes:]
 
 
-def pack_kernel(v_ref, out_ref, first_ref, last_ref):
-    _, span, merged = v_ref.shape
-    c = pl.program_id(0)
+def pack_kernel(v_ref, out_ref, first_ref, last_ref, held, sems):
+    comps, span, merged = v_ref.shape
     pairs = merged // (2 * LANES)
     groups = out_ref.shape[0] // LANES
-    for q in range(pairs):
-        at = q * 2 * LANES
-        both = jnp.concatenate([v_ref[0, :, at : at + LANES], v_ref[0, :, at + LANES : at + 2 * LANES]], axis=0)
-        out_ref[pl.ds(c * pairs + q, LANES, stride=groups), :] = both.T
-    first_ref[pl.ds(c, 1), :] = v_ref[0, 0:1, :]
-    last_ref[pl.ds(c, 1), :] = v_ref[0, span - 1 : span, :]
-
-
-def smooth_kernel(x_ref, f_ref, r_ref, e_ref, b_ref, cos_ref, sin_ref, out_ref):
+    steps = sems.shape[0]
+    width = merged // steps
+    loads = []
+    for i in range(steps):
+        piece = (slice(None), slice(None), pl.ds(i * width, width))
+        loads.append(pltpu.make_async_copy(v_ref.at[piece], held.at[piece], sems.at[i]))
+        loads[-1].start()
+    for i in range(steps):
+        loads[i].wait()
+        for q in range(i * pairs // steps, (i + 1) * pairs // steps):
+            at = q * 2 * LANES
+            for c in range(comps):
+                both = jnp.concatenate([held[c, :, at : at + LANES], held[c, :, at + LANES : at + 2 * LANES]], axis=0)
+                out_ref[pl.ds(c * pairs + q, LANES, stride=groups), :] = both.T
+    for c in range(comps):
+        first_ref[c : c + 1, :] = held[c, 0:1, :]
+        last_ref[c : c + 1, :] = held[c, span - 1 : span, :]
+
+
+def smooth_kernel(x_ref, f_ref, r_ref, e_ref, b_ref, cos_ref, sin_ref, out_ref, z_ref, w_ref, lone_ref):
     devices = f_ref.shape[0] // 2
     half = devices // 2
     groups = x_ref.shape[0] // devices
-    cos, sin = cos_ref[...], sin_ref[...]
-    forward, inner, backward = f_ref[...], r_ref[...], b_ref[...]
-    for p in range(0, groups, 2):
+
+    def outer(p):
+        cos, sin = cos_ref[...], sin_ref[...]
         pair = [x_ref[pl.ds(p + i, devices, stride=groups), :] for i in range(2)]
-        y = dot_rows(forward, jnp.concatenate(pair, axis=1))
-        turned = []
+        y = dot_rows(f_ref[...], jnp.concatenate(pair, axis=1))
         for i in range(2):
+            at = (p + i) * devices
             re = y[:half, i * LANES : (i + 1) * LANES]
             im = y[half:, i * LANES : (i + 1) * LANES]
-            turned += [re * cos + im * sin, im * cos - re * sin]
-        w = dot_lanes(jnp.concatenate(turned, axis=0), inner)
-        lone = dot_lanes(jnp.concatenate([y[0:8, :LANES], y[0:8, LANES:]], axis=0), e_ref[...])
-        back = []
+            z_ref[at : at + half, :] = re * cos + im * sin
+            z_ref[at + half : at + devices, :] = im * cos - re * sin
+
+    def inner(p):
+        cos, sin = cos_ref[...], sin_ref[...]
+        w = dot_lanes(z_ref[p * devices : (p + 2) * devices, :], r_ref[...])
         for i in range(2):
+            at = (p + i) * LANES
             re = w[i * devices : i * devices + half]
             im = w[i * devices + half : (i + 1) * devices]
-            first = lax.broadcasted_iota(jnp.int32, (8, LANES), 0) == 0
-            top = re * cos - im * sin
-            top = jnp.concatenate([top[:8] + jnp.where(first, lone[i * 8 : (i + 1) * 8], 0.0), top[8:]], axis=0)
-            back.append(jnp.concatenate([top, im * cos + re * sin], axis=0))
-        y = dot_rows(backward, jnp.concatenate(back, axis=1))
+            w_ref[:half, at : at + LANES] = re * cos - im * sin
+            w_ref[half:, at : at + LANES] = im * cos + re * sin
+
+    def extra():
+        rows = [z_ref[p * devices : p * devices + 1, :] for p in range(groups)]
+        rows.append(jnp.zeros((-groups % 8, LANES), jnp.float32))
+        lone = dot_lanes(jnp.concatenate(rows, axis=0), e_ref[...]) * (2.0 / devices)
+        for p in range(groups):
+            lone_ref[:, p * LANES : (p + 1) * LANES] = lone[p : p + 1]
+
+    def outer_back(p):
+        both = slice(p * LANES, (p + 2) * LANES)
+        y = dot_rows(b_ref[...], w_ref[:, both]) + lone_ref[:, both]
         for i in range(2):
             out_ref[pl.ds(p + i, devices, stride=groups), :] = y[:, i * LANES : (i + 1) * LANES]
 
-
-def forcing_kernel(v_ref, before_ref, after_ref, flow_ref, slope_ref, mask_ref, place_ref, out_ref, *, normal):
+    for p in range(0, groups + 2, 2):
+        if p < groups:
+            outer(p)
+        if p >= 2:
+            inner(p - 2)
+    extra()
+    for p in range(0, groups, 2):
+        outer_back(p)
+
+
+def forcing_kernel(v_ref, flow_ref, slope_ref, mask_ref, place_ref, out_ref, gain_ref, *, normal):
     comps, span, merged = v_ref.shape
     lane = lax.broadcasted_iota(jnp.int32, (1, merged), 1)
     row = lax.rem(lane, normal)
@@ -135,6 +165,9 @@
     )
     flow = -0.25 * flow_ref[...]
     slope = 0.25 * slope_ref[...]
+    nothing = jnp.zeros((1, merged), jnp.float32)
+    gain_ref[0:1, :] = 0.15 * solid[0:1]
+    gain_ref[1:2, :] = 0.15 * solid[span - 1 : span]
     for c in range(comps):
         v = v_ref[c]
         ahead = pltpu.roll(v, merged - normal, 1)
@@ -144,23 +177,30 @@
         total = flow * (ahead - behind) + 0.05 * (ahead + behind + upper + lower - 4.0 * v)
         if c == 0:
             total = total - slope * v_ref[1]
-        plus = jnp.concatenate([v[1:], after_ref[c : c + 1, :]], axis=0)
-        minus = jnp.concatenate([before_ref[c : c + 1, :], v[:-1]], axis=0)
+        plus = jnp.concatenate([v[1:], nothing], axis=0)
+        minus = jnp.concatenate([nothing, v[:-1]], axis=0)
         total = total + solid * (0.15 * (plus + minus - 2.0 * v) - 0.4 * v)
         out_ref[c] = total - v
 
 
-def unpack_kernel(s_ref, f_ref, out_ref):
-    _, span, merged = out_ref.shape
-    c = pl.program_id(0)
+def unpack_kernel(s_ref, f_ref, gain_ref, before_ref, after_ref, out_ref, held, sems):
+    comps, span, merged = f_ref.shape
     pairs = merged // (2 * LANES)
     groups = s_ref.shape[0] // LANES
-    for q in range(pairs):
-        both = s_ref[pl.ds(c * pairs + q, LANES, stride=groups), :].T
-        lo = slice(q * 2 * LANES, q * 2 * LANES + LANES)
-        hi = slice(q * 2 * LANES + LANES, (q + 1) * 2 * LANES)
-        out_ref[0, :, lo] = f_ref[c, :, lo] + both[:span]
-        out_ref[0, :, hi] = f_ref[c, :, hi] + both[span:]
+    stores = []
+    for c in range(comps):
+        for q in range(pairs):
+            both = s_ref[pl.ds(c * pairs + q, LANES, stride=groups), :].T
+            lo = slice(q * 2 * LANES, q * 2 * LANES + LANES)
+            hi = slice(q * 2 * LANES + LANES, (q + 1) * 2 * LANES)
+            held[c, :, lo] = f_ref[c, :, lo] + both[:span]
+            held[c, :, hi] = f_ref[c, :, hi] + both[span:]
+        held[c, 0:1, :] = held[c, 0:1, :] + gain_ref[0:1, :] * before_ref[c : c + 1, :]
+        held[c, span - 1 : span, :] = held[c, span - 1 : span, :] + gain_ref[1:2, :] * after_ref[c : c + 1, :]
+        stores.append(pltpu.make_async_copy(held.at[c], out_ref.at[c], sems.at[c]))
+        stores[-1].start()
+    for store in stores:
+        store.wait()
 
 
 def exchange(rows, devices):
@@ -181,44 +221,51 @@
     groups = comps * merged // devices // (LANES // span)
     f32 = jnp.float32
     here = pl.BlockSpec(memory_space=pltpu.VMEM)
-    part = pl.BlockSpec((1, span, merged), lambda c: (c, 0, 0))
+    away = pl.BlockSpec(memory_space=pltpu.HBM)
     edge = pltpu.VMEM((comps, merged), f32)
     rows = pltpu.VMEM((devices * groups, LANES), f32)
     v = jnp.transpose(velocity, (1, 0, 2))
     sent, first, last = pl.pallas_call(
-        pack_kernel, grid=(comps,), in_specs=[part], out_specs=(here,) * 3, out_shape=(rows, edge, edge)
+        pack_kernel,
+        in_specs=[away],
+        out_specs=(here,) * 3,
+        out_shape=(rows, edge, edge),
+        scratch_shapes=[pltpu.VMEM(v.shape, f32), pltpu.SemaphoreType.DMA((3,))],
     )(v)
     got = exchange(sent, devices)
-    before = lax.ppermute(last, AXES, [(i, (i + 1) % devices) for i in range(devices)])
-    after = lax.ppermute(first, AXES, [((i + 1) % devices, i) for i in range(devices)])
-    got, before, after = lax.optimization_barrier((got, before, after))
     smoothed = pl.pallas_call(
         smooth_kernel,
         in_specs=[here] * 7,
         out_specs=here,
         out_shape=rows,
-        cost_estimate=pl.CostEstimate(flops=0, bytes_accessed=10_000_000, transcendentals=0),
+        scratch_shapes=[
+            pltpu.VMEM((groups * devices, LANES), f32),
+            pltpu.VMEM((devices, groups * LANES), f32),
+            pltpu.VMEM((1, groups * LANES), f32),
+        ],
     )(in_vmem(got), *(in_vmem(jnp.asarray(t)) for t in tables(devices, span)))
     back = exchange(smoothed, devices)
+    before = lax.ppermute(last, AXES, [(i, (i + 1) % devices) for i in range(devices)])
+    after = lax.ppermute(first, AXES, [((i + 1) % devices, i) for i in range(devices)])
     padded = jnp.pad(base_flow, 1)
     flow = jnp.tile(base_flow, planes)[None]
     slope = jnp.tile(padded[2:] - padded[:-2], planes)[None]
     lane = np.arange(merged) % normal
     place = jnp.asarray((lane[None, :] == np.arange(wall_rows)[:, None]).astype(ml_dtypes.bfloat16))
-    forcing = pl.pallas_call(
+    forcing, gain = pl.pallas_call(
         functools.partial(forcing_kernel, normal=normal),
-        in_specs=[here] * 7,
-        out_specs=here,
-        out_shape=pltpu.VMEM(v.shape, f32),
+        in_specs=[here] * 5,
+        out_specs=(here,) * 2,
+        out_shape=(pltpu.VMEM(v.shape, f32), pltpu.VMEM((2, merged), f32)),
         cost_estimate=pl.CostEstimate(flops=0, bytes_accessed=10_000_000, transcendentals=0),
-    )(v, in_vmem(before), in_vmem(after), flow, slope, slot_mask, place)
+    )(v, flow, slope, slot_mask, place)
     out = pl.pallas_call(
         unpack_kernel,
-        grid=(comps,),
-        in_specs=[here] * 2,
-        out_specs=part,
+        in_specs=[here] * 5,
+        out_specs=away,
         out_shape=jax.ShapeDtypeStruct(v.shape, f32),
-    )(in_vmem(back), in_vmem(forcing))
+        scratch_shapes=[pltpu.VMEM(v.shape, f32), pltpu.SemaphoreType.DMA((comps,))],
+    )(in_vmem(back), in_vmem(forcing), in_vmem(gain), in_vmem(before), in_vmem(after))
     return jnp.transpose(out, (1, 0, 2))
 
 

time: 67.3 us -> 62.7 us (0.932)
  blocking collectives: 0 us -> 31.5 us
  waiting for transfers between devices: 29.9 us -> 9.34 us
  starting transfers between devices: 23.1 us -> 12 us
  Pallas kernels: 11.9 us -> 7.82 us
    all_to_all x0 -> x1, blocking collectives: none -> 31.5 us  [exchange(): lax.all_to_all(rows.reshape(devices, 1, -1), AXES, split_axis=0, concat_a...]
    all_to_all x2 -> x1, waiting for transfers between devices: 17.1 us -> 0.82 us  [exchange(): lax.all_to_all(rows.reshape(devices, 1, -1), AXES, split_axis=0, concat_a...]
    all_to_all x2 -> x1, starting transfers between devices: 15.9 us -> 4.76 us  [exchange(): lax.all_to_all(rows.reshape(devices, 1, -1), AXES, split_axis=0, concat_a...]
    ppermute x1, waiting for transfers between devices: 12.8 us -> 8.52 us  [body(): lax.ppermute(last, AXES, [(i, (i + 1) % devices) for i in range(devices)])]
    pallas_call x2, Pallas kernels: 5.17 us -> 2.75 us  [the longest x1 1.54 us: body(): pl.pallas_call(pack_kernel, in_specs=[away], out_specs=(here,) * 3, out_s...]
    pallas_call x1, Pallas kernels: 3.9 us -> 2.29 us  [body(): pl.pallas_call(smooth_kernel, in_specs=[here] * 7, out_specs=here, out_sh...]
  transfers between devices with their start and end apart: 4 -> 3, of which waited for: 3 -> 2; matrix products, arithmetic and copies ran while one was open for 2% -> 2% of each run, Pallas kernels for 4% -> 4%
where the time goes in v2:
time: 62.7 us; the launch traced here: 62.3 us
  blocking collectives  31.5 us (50%)
  starting transfers between devices  12 us (19%)
  waiting for transfers between devices  9.34 us (15%)
  Pallas kernels  7.82 us (12%)
  local copies, waits for them, and re-layouts  1.4 us (2%)
    all_to_all x1, blocking collectives, exchange(): lax.all_to_all(rows.reshape(devices, 1, -1), AXES, split_axis=0, concat_a...  31.5 us
    ppermute x1, waiting for transfers between devices, body(): lax.ppermute(last, AXES, [(i, (i + 1) % devices) for i in range(devices)])  8.52 us
    ppermute x1, starting transfers between devices, body(): lax.ppermute(first, AXES, [((i + 1) % devices, i) for i in range(devices)])  7.16 us
    all_to_all x1, starting transfers between devices, exchange(): lax.all_to_all(rows.reshape(devices, 1, -1), AXES, split_axis=0, concat_a...  4.76 us
    pallas_call x1, Pallas kernels, body(): pl.pallas_call(functools.partial(forcing_kernel, normal=normal), in_specs...  2.79 us
    pallas_call x1, Pallas kernels, body(): pl.pallas_call(smooth_kernel, in_specs=[here] * 7, out_specs=here, out_sh...  2.29 us
    pallas_call x1, Pallas kernels, body(): pl.pallas_call(pack_kernel, in_specs=[away], out_specs=(here,) * 3, out_s...  1.54 us
  transfers between devices with their start and end apart: 3, of which 2 were waited for; matrix products, arithmetic and copies ran while one was open for 2% of the time, Pallas kernels for 4%

profile of v2, /device:TPU:0, one launch (start us, length us, event | category | flops | bytes accessed | tf_op | source)
XLA Modules:
  0.0 62.3 jit_solution(1083755353038255070)
XLA Ops:
  0.0 1.5 %shard_map.100 = (f32[2304,128]{1,0:T(8,128)S(1)}, f32[3,1536]{1,0:T(4,128)S(1)}, f32[3,1536]{1,0:T(4,128)S(1)}) custom-call(f32[3,64,1536]{2,1,0:T(8,128)} %bitcast.9), custom_call_target="tpu_custom_call" | custom-call | tf_op jit(solution)/shard_map/pallas_call | solution.py:228
  1.5 0.0 copy-start
  1.6 0.0 copy-start.1
  1.6 0.0 copy-start.2
  1.6 0.0 copy-start.3
  1.6 0.0 copy-start.4
  1.6 0.0 copy-start.5
  1.6 31.5 %all_to_all.10 = f32[128,1,2304]{2,1,0:T(1,128)S(1)} all-to-all(f32[128,1,2304]{2,1,0:T(1,128)S(1)} %bitcast.8), channel_id=1, replica_groups=mesh['zc'=16,'zl'=8] {'zc','zl'}, dimensions={0} | all-to-all | bytes 2359296 | tf_op jit(solution)/shard_map/all_to_all | solution.py:207
  33.1 0.0 copy-done
  33.1 0.0 copy-done.1
  33.1 0.0 copy-done.2
  33.1 0.0 copy-done.3
  33.1 0.0 copy-done.4
  33.2 0.0 copy-done.5
  33.2 2.3 %shard_map.101 = f32[2304,128]{1,0:T(8,128)} custom-call(f32[2304,128]{1,0:T(8,128)S(1)} %bitcast.7, bf16[256,256]{1,0:T(8,128)(2,1)S(1)} %copy-done, bf16[256,256]{1,0:T(8,128)(2,1)S(1)} %copy-done.1, bf16[256,256]{1,0:T(8,128)(2,1)S(1)} %copy-done.2, bf16[256,256]{1,0:T(8,128)(2,1)S(1)} %copy-done.3, f32[64,128]{1,0:T(8,128)S(1)} %copy-done.4, ...), custom_call_target="tpu_custom_call" | custom-call | tf_op jit(solution)/shard_map/pallas_call | solution.py:236
  35.5 0.0 copy-start.6
  35.5 4.8 %all-to-all-start.1 = ((f32[128,1,2304]{2,1,0:T(1,128)}), f32[128,1,2304]{2,1,0:T(1,128)S(1)}, u32[]{:S(2)}, u32[]{:S(2)}) async-start(f32[128,1,2304]{2,1,0:T(1,128)} %bitcast.3), calls=%async_computation.1 | async-start | bytes 2359296 | tf_op jit(solution)/shard_map/all_to_all | solution.py:207
  40.2 0.1 collective-permute-start
  40.3 7.2 %collective-permute-start.1 = (f32[3,1536]{1,0:T(4,128)S(1)}, f32[3,1536]{1,0:T(4,128)S(1)}, u32[]{:S(2)}, u32[]{:S(2)}) collective-permute-start(f32[3,1536]{1,0:T(4,128)S(1)} %get-tuple-element.14), channel_id=1, source_target_pairs={{1,0},{2,1},{3,2},{4,3},{5,4},{6,5},{7,6},{8,7},{9,8},{10,9},{11,1... | collective-permute-start | bytes 55304 | tf_op jit(solution)/shard_map/ppermute | solution.py:249
  47.5 0.0 copy-done.6
  47.5 0.1 slice_subtract_fusion
  47.6 0.7 %broadcast_in_dim_tile.7.slope_ref = f32[1,1536]{1,0:T(1,128)} reshape(f32[8,192]{1,0:T(8,128)S(1)} %tile.5) | data formatting | bytes 12288 | tf_op jit(solution)/shard_map/broadcast_in_dim;tile | solution.py:252
  48.2 0.7 %broadcast_in_dim_tile.6.flow_ref = f32[1,1536]{1,0:T(1,128)} reshape(f32[8,192]{1,0:T(8,128)S(1)} %tile.4) | data formatting | bytes 12288 | tf_op jit(solution)/shard_map/broadcast_in_dim;tile | solution.py:251
  48.9 2.8 %shard_map.102 = (f32[3,64,1536]{2,1,0:T(8,128)S(1)}, f32[2,1536]{1,0:T(2,128)S(1)}) custom-call(f32[3,64,1536]{2,1,0:T(8,128)} %bitcast.10, f32[1,1536]{1,0:T(1,128)} %broadcast_in_dim_tile.6.flow_ref, f32[1,1536]{1,0:T(1,128)} %broadcast_in_dim_tile.7.slope_ref, s32[8,64]{1,0:T(8,128)} %mask_ref.1, bf16[8,1536]{1,0:T(8,128)(2,1)} %constant.23.clone.place_ref), custom_call_target="tpu_custom_call" | custom-call | bytes 10000000 | tf_op jit(solution)/shard_map/pallas_call | solution.py:255
  51.7 8.5 %collective-permute-done.before_ref = f32[3,1536]{1,0:T(4,128)S(1)} collective-permute-done((f32[3,1536]{1,0:T(4,128)S(1)}, f32[3,1536]{1,0:T(4,128)S(1)}, u32[]{:S(2)}, u32[]{:S(2)}) %collective-permute-start) | collective-permute-done | bytes 18464 | tf_op jit(solution)/shard_map/ppermute | solution.py:248
  60.2 0.0 collective-permute-done.1.after_ref
  60.2 0.8 %all-to-all-done.1 = f32[128,1,2304]{2,1,0:T(1,128)S(1)} async-done(((f32[128,1,2304]{2,1,0:T(1,128)}), f32[128,1,2304]{2,1,0:T(1,128)S(1)}, u32[]{:S(2)}, u32[]{:S(2)}) %all-to-all-start.1) | async-done | bytes 1179680 | tf_op jit(solution)/shard_map/all_to_all | solution.py:207
  61.0 1.2 %shard_map.103 = f32[3,64,1536]{2,1,0:T(8,128)} custom-call(f32[2304,128]{1,0:T(8,128)S(1)} %bitcast.6, f32[3,64,1536]{2,1,0:T(8,128)S(1)} %get-tuple-element.11.f_ref, f32[2,1536]{1,0:T(2,128)S(1)} %get-tuple-element.12.gain_ref, f32[3,1536]{1,0:T(4,128)S(1)} %collective-permute-done.before_ref, f32[3,1536]{1,0:T(4,128)S(1)} %collective-permute-done.1.after_ref), custom_call_target="tpu_custom_call" | custom-call | tf_op jit(solution)/shard_map/pallas_call | solution.py:262
  (2 shorter events, 0.0 us)
Async XLA Ops:
  1.5 31.6 %copy-start = (bf16[256,256]{1,0:T(8,128)(2,1)S(1)}, bf16[256,256]{1,0:T(8,128)(2,1)}, u32[]{:S(2)}) copy-start(bf16[256,256]{1,0:T(8,128)(2,1)} %constant.17.clone.f_ref) | copy-start | bytes 393220
  1.6 31.6 %copy-start.1 = (bf16[256,256]{1,0:T(8,128)(2,1)S(1)}, bf16[256,256]{1,0:T(8,128)(2,1)}, u32[]{:S(2)}) copy-start(bf16[256,256]{1,0:T(8,128)(2,1)} %constant.18.clone.r_ref) | copy-start | bytes 393220
  1.6 31.6 %copy-start.2 = (bf16[256,256]{1,0:T(8,128)(2,1)S(1)}, bf16[256,256]{1,0:T(8,128)(2,1)}, u32[]{:S(2)}) copy-start(bf16[256,256]{1,0:T(8,128)(2,1)} %constant.19.clone.e_ref) | copy-start | bytes 393220
  1.6 31.6 %copy-start.3 = (bf16[256,256]{1,0:T(8,128)(2,1)S(1)}, bf16[256,256]{1,0:T(8,128)(2,1)}, u32[]{:S(2)}) copy-start(bf16[256,256]{1,0:T(8,128)(2,1)} %constant.20.clone.b_ref) | copy-start | bytes 393220
  1.6 31.6 %copy-start.4 = (f32[64,128]{1,0:T(8,128)S(1)}, f32[64,128]{1,0:T(8,128)}, u32[]{:S(2)}) copy-start(f32[64,128]{1,0:T(8,128)} %constant.21.clone.cos_ref) | copy-start | bytes 98308
  1.6 31.5 %copy-start.5 = (f32[64,128]{1,0:T(8,128)S(1)}, f32[64,128]{1,0:T(8,128)}, u32[]{:S(2)}) copy-start(f32[64,128]{1,0:T(8,128)} %constant.22.clone.sin_ref) | copy-start | bytes 98308
  35.5 12.0 %copy-start.6 = (f32[192]{0:T(256)S(1)}, f32[192]{0:T(256)}, u32[]{:S(2)}) copy-start(f32[192]{0:T(256)} %param.11) | copy-start | bytes 2308
  35.5 25.6 %all-to-all-start.1 = ((f32[128,1,2304]{2,1,0:T(1,128)}), f32[128,1,2304]{2,1,0:T(1,128)S(1)}, u32[]{:S(2)}, u32[]{:S(2)}) async-start(f32[128,1,2304]{2,1,0:T(1,128)} %bitcast.3), calls=%async_computation.1 | async-start | bytes 2359296 | tf_op jit(solution)/shard_map/all_to_all | solution.py:207
  40.2 20.0 %collective-permute-start = (f32[3,1536]{1,0:T(4,128)S(1)}, f32[3,1536]{1,0:T(4,128)S(1)}, u32[]{:S(2)}, u32[]{:S(2)}) collective-permute-start(f32[3,1536]{1,0:T(4,128)S(1)} %get-tuple-element.13), channel_id=1, source_target_pairs={{0,1},{1,2},{2,3},{3,4},{4,5},{5,6},{6,7},{7,8},{8,9},{9,10},{10,1... | collective-permute-start | bytes 55304 | tf_op jit(solution)/shard_map/ppermute | solution.py:248
  40.3 19.9 %collective-permute-start.1 = (f32[3,1536]{1,0:T(4,128)S(1)}, f32[3,1536]{1,0:T(4,128)S(1)}, u32[]{:S(2)}, u32[]{:S(2)}) collective-permute-start(f32[3,1536]{1,0:T(4,128)S(1)} %get-tuple-element.14), channel_id=1, source_target_pairs={{1,0},{2,1},{3,2},{4,3},{5,4},{6,5},{7,6},{8,7},{9,8},{10,9},{11,1... | collective-permute-start | bytes 55304 | tf_op jit(solution)/shard_map/ppermute | solution.py:249

commit v3 on v2

--- a/solution.py
+++ b/solution.py
@@ -11,7 +11,8 @@
 from jax.sharding import PartitionSpec as P
 
 LANES = 128
-AXES = ("zc", "zl")
+AXES = ("y", "z", "x", "core")
+RANKS = ("core", "z", "x", "y")
 
 
 def split_const(table):
@@ -21,10 +22,11 @@
 
 
 @functools.cache
-def tables(devices, span):
+def tables(sizes, span):
+    devices = math.prod(sizes)
     length = devices * span
     half = devices // 2
-    d = np.arange(devices)
+    d = np.arange(devices).reshape(sizes).transpose([AXES.index(a) for a in RANKS]).reshape(-1)
     k = np.arange(half)
     turn = 2.0 * math.pi * (k[:, None] * d[None, :] % devices) / devices
     forward = np.concatenate([np.cos(turn), -np.sin(turn)], axis=0)
@@ -204,7 +206,7 @@
 
 
 def exchange(rows, devices):
-    spread = lax.all_to_all(rows.reshape(devices, 1, -1), AXES, split_axis=0, concat_axis=0, tiled=True)
+    spread = lax.all_to_all(rows.reshape(devices, 1, -1), RANKS, split_axis=0, concat_axis=0, tiled=True)
     return spread.reshape(rows.shape)
 
 
@@ -217,7 +219,8 @@
     normal = base_flow.shape[0]
     planes = merged // normal
     wall_rows = slot_mask.shape[0]
-    devices = lax.axis_size(AXES)
+    sizes = tuple(lax.axis_size(a) for a in AXES)
+    devices = math.prod(sizes)
     groups = comps * merged // devices // (LANES // span)
     f32 = jnp.float32
     here = pl.BlockSpec(memory_space=pltpu.VMEM)
@@ -243,7 +246,7 @@
             pltpu.VMEM((devices, groups * LANES), f32),
             pltpu.VMEM((1, groups * LANES), f32),
         ],
-    )(in_vmem(got), *(in_vmem(jnp.asarray(t)) for t in tables(devices, span)))
+    )(in_vmem(got), *(in_vmem(jnp.asarray(t)) for t in tables(sizes, span)))
     back = exchange(smoothed, devices)
     before = lax.ppermute(last, AXES, [(i, (i + 1) % devices) for i in range(devices)])
     after = lax.ppermute(first, AXES, [((i + 1) % devices, i) for i in range(devices)])
@@ -270,6 +273,9 @@
 
 
 def solution(mesh):
+    outer, inner = mesh.devices.shape
+    side = inner // 2
+    torus = jax.sharding.Mesh(mesh.devices.reshape(outer // side, side, side, 2), AXES)
     in_specs = (P(AXES, None, None), P(), P(None, AXES))
     out_specs = P(AXES, None, None)
-    return jax.shard_map(body, mesh=mesh, in_specs=in_specs, out_specs=out_specs, check_vma=False)
+    return jax.shard_map(body, mesh=torus, in_specs=in_specs, out_specs=out_specs, check_vma=False)

time: 62.7 us -> 61.4 us (0.979)
  blocking collectives: 31.5 us -> 30.3 us
  starting transfers between devices: 12 us -> 12.7 us
    all_to_all x1, blocking collectives: 31.5 us -> 30.3 us  [exchange(): lax.all_to_all(rows.reshape(devices, 1, -1), RANKS, split_axis=0, concat_...]
    all_to_all x1, waiting for transfers between devices: 0.82 us -> 0.01 us  [exchange(): lax.all_to_all(rows.reshape(devices, 1, -1), RANKS, split_axis=0, concat_...]
    all_to_all x1, starting transfers between devices: 4.76 us -> 5.44 us  [exchange(): lax.all_to_all(rows.reshape(devices, 1, -1), RANKS, split_axis=0, concat_...]
  transfers between devices with their start and end apart: 3 -> 3, of which waited for: 2 -> 1; matrix products, arithmetic and copies ran while one was open for 2% -> 2% of each run, Pallas kernels for 4% -> 5%
where the time goes in v3:
time: 61.4 us; the launch traced here: 61.1 us
  blocking collectives  30.3 us (49%)
  starting transfers between devices  12.7 us (21%)
  waiting for transfers between devices  8.76 us (14%)
  Pallas kernels  7.83 us (13%)
  local copies, waits for them, and re-layouts  1.4 us (2%)
    all_to_all x1, blocking collectives, exchange(): lax.all_to_all(rows.reshape(devices, 1, -1), RANKS, split_axis=0, concat_...  30.3 us
    ppermute x1, waiting for transfers between devices, body(): lax.ppermute(last, AXES, [(i, (i + 1) % devices) for i in range(devices)])  8.75 us
    ppermute x1, starting transfers between devices, body(): lax.ppermute(first, AXES, [((i + 1) % devices, i) for i in range(devices)])  7.16 us
    all_to_all x1, starting transfers between devices, exchange(): lax.all_to_all(rows.reshape(devices, 1, -1), RANKS, split_axis=0, concat_...  5.44 us
    pallas_call x1, Pallas kernels, body(): pl.pallas_call(functools.partial(forcing_kernel, normal=normal), in_specs...  2.79 us
    pallas_call x1, Pallas kernels, body(): pl.pallas_call(smooth_kernel, in_specs=[here] * 7, out_specs=here, out_sh...  2.29 us
    pallas_call x1, Pallas kernels, body(): pl.pallas_call(pack_kernel, in_specs=[away], out_specs=(here,) * 3, out_s...  1.54 us
  transfers between devices with their start and end apart: 3, of which 1 were waited for; matrix products, arithmetic and copies ran while one was open for 2% of the time, Pallas kernels for 5%

profile of v3, /device:TPU:0, one launch (start us, length us, event | category | flops | bytes accessed | tf_op | source)
XLA Modules:
  0.0 61.1 jit_solution(1700853896949624400)
XLA Ops:
  0.0 1.5 %shard_map.100 = (f32[2304,128]{1,0:T(8,128)S(1)}, f32[3,1536]{1,0:T(4,128)S(1)}, f32[3,1536]{1,0:T(4,128)S(1)}) custom-call(f32[3,64,1536]{2,1,0:T(8,128)} %bitcast.9), custom_call_target="tpu_custom_call" | custom-call | tf_op jit(solution)/shard_map/pallas_call | solution.py:231
  1.5 0.0 copy-start
  1.6 0.0 copy-start.1
  1.6 0.0 copy-start.2
  1.6 0.0 copy-start.3
  1.6 0.0 copy-start.4
  1.6 0.0 copy-start.5
  1.6 30.3 %all_to_all.10 = f32[128,1,2304]{2,1,0:T(1,128)S(1)} all-to-all(f32[128,1,2304]{2,1,0:T(1,128)S(1)} %bitcast.8), channel_id=1, replica_groups=mesh['y'=4,'z'=4,'x'=4,'core'=2] {'core','z','x','y'}, dimensions={0} | all-to-all | bytes 2359296 | tf_op jit(solution)/shard_map/all_to_all | solution.py:209
  31.9 0.0 copy-done
  31.9 0.0 copy-done.1
  31.9 0.0 copy-done.2
  31.9 0.0 copy-done.3
  31.9 0.0 copy-done.4
  31.9 0.0 copy-done.5
  31.9 2.3 %shard_map.101 = f32[2304,128]{1,0:T(8,128)} custom-call(f32[2304,128]{1,0:T(8,128)S(1)} %bitcast.7, bf16[256,256]{1,0:T(8,128)(2,1)S(1)} %copy-done, bf16[256,256]{1,0:T(8,128)(2,1)S(1)} %copy-done.1, bf16[256,256]{1,0:T(8,128)(2,1)S(1)} %copy-done.2, bf16[256,256]{1,0:T(8,128)(2,1)S(1)} %copy-done.3, f32[64,128]{1,0:T(8,128)S(1)} %copy-done.4, ...), custom_call_target="tpu_custom_call" | custom-call | tf_op jit(solution)/shard_map/pallas_call | solution.py:239
  34.2 0.0 copy-start.6
  34.2 5.4 %all-to-all-start.1 = ((f32[128,1,2304]{2,1,0:T(1,128)}), f32[128,1,2304]{2,1,0:T(1,128)S(1)}, u32[]{:S(2)}, u32[]{:S(2)}) async-start(f32[128,1,2304]{2,1,0:T(1,128)} %bitcast.3), calls=%async_computation.1 | async-start | bytes 2359296 | tf_op jit(solution)/shard_map/all_to_all | solution.py:209
  39.7 0.1 collective-permute-start
  39.8 7.2 %collective-permute-start.1 = (f32[3,1536]{1,0:T(4,128)S(1)}, f32[3,1536]{1,0:T(4,128)S(1)}, u32[]{:S(2)}, u32[]{:S(2)}) collective-permute-start(f32[3,1536]{1,0:T(4,128)S(1)} %get-tuple-element.14), channel_id=1, source_target_pairs={{1,0},{2,1},{3,2},{4,3},{5,4},{6,5},{7,6},{8,7},{9,8},{10,9},{11,1... | collective-permute-start | bytes 55304 | tf_op jit(solution)/shard_map/ppermute | solution.py:252
  46.9 0.0 copy-done.6
  46.9 0.1 slice_subtract_fusion
  47.0 0.7 %broadcast_in_dim_tile.7.slope_ref = f32[1,1536]{1,0:T(1,128)} reshape(f32[8,192]{1,0:T(8,128)S(1)} %tile.5) | data formatting | bytes 12288 | tf_op jit(solution)/shard_map/broadcast_in_dim;tile | solution.py:255
  47.7 0.7 %broadcast_in_dim_tile.6.flow_ref = f32[1,1536]{1,0:T(1,128)} reshape(f32[8,192]{1,0:T(8,128)S(1)} %tile.4) | data formatting | bytes 12288 | tf_op jit(solution)/shard_map/broadcast_in_dim;tile | solution.py:254
  48.4 2.8 %shard_map.102 = (f32[3,64,1536]{2,1,0:T(8,128)S(1)}, f32[2,1536]{1,0:T(2,128)S(1)}) custom-call(f32[3,64,1536]{2,1,0:T(8,128)} %bitcast.10, f32[1,1536]{1,0:T(1,128)} %broadcast_in_dim_tile.6.flow_ref, f32[1,1536]{1,0:T(1,128)} %broadcast_in_dim_tile.7.slope_ref, s32[8,64]{1,0:T(8,128)} %mask_ref.1, bf16[8,1536]{1,0:T(8,128)(2,1)} %constant.23.clone.place_ref), custom_call_target="tpu_custom_call" | custom-call | bytes 10000000 | tf_op jit(solution)/shard_map/pallas_call | solution.py:258
  51.1 8.8 %collective-permute-done.before_ref = f32[3,1536]{1,0:T(4,128)S(1)} collective-permute-done((f32[3,1536]{1,0:T(4,128)S(1)}, f32[3,1536]{1,0:T(4,128)S(1)}, u32[]{:S(2)}, u32[]{:S(2)}) %collective-permute-start) | collective-permute-done | bytes 18464 | tf_op jit(solution)/shard_map/ppermute | solution.py:251
  59.9 0.0 collective-permute-done.1.after_ref
  59.9 0.0 all-to-all-done.1
  59.9 1.2 %shard_map.103 = f32[3,64,1536]{2,1,0:T(8,128)} custom-call(f32[2304,128]{1,0:T(8,128)S(1)} %bitcast.6, f32[3,64,1536]{2,1,0:T(8,128)S(1)} %get-tuple-element.11.f_ref, f32[2,1536]{1,0:T(2,128)S(1)} %get-tuple-element.12.gain_ref, f32[3,1536]{1,0:T(4,128)S(1)} %collective-permute-done.before_ref, f32[3,1536]{1,0:T(4,128)S(1)} %collective-permute-done.1.after_ref), custom_call_target="tpu_custom_call" | custom-call | tf_op jit(solution)/shard_map/pallas_call | solution.py:265
  (2 shorter events, 0.0 us)
Async XLA Ops:
  1.5 30.3 %copy-start = (bf16[256,256]{1,0:T(8,128)(2,1)S(1)}, bf16[256,256]{1,0:T(8,128)(2,1)}, u32[]{:S(2)}) copy-start(bf16[256,256]{1,0:T(8,128)(2,1)} %constant.17.clone.f_ref) | copy-start | bytes 393220
  1.6 30.3 %copy-start.1 = (bf16[256,256]{1,0:T(8,128)(2,1)S(1)}, bf16[256,256]{1,0:T(8,128)(2,1)}, u32[]{:S(2)}) copy-start(bf16[256,256]{1,0:T(8,128)(2,1)} %constant.18.clone.r_ref) | copy-start | bytes 393220
  1.6 30.3 %copy-start.2 = (bf16[256,256]{1,0:T(8,128)(2,1)S(1)}, bf16[256,256]{1,0:T(8,128)(2,1)}, u32[]{:S(2)}) copy-start(bf16[256,256]{1,0:T(8,128)(2,1)} %constant.19.clone.e_ref) | copy-start | bytes 393220
  1.6 30.3 %copy-start.3 = (bf16[256,256]{1,0:T(8,128)(2,1)S(1)}, bf16[256,256]{1,0:T(8,128)(2,1)}, u32[]{:S(2)}) copy-start(bf16[256,256]{1,0:T(8,128)(2,1)} %constant.20.clone.b_ref) | copy-start | bytes 393220
  1.6 30.3 %copy-start.4 = (f32[64,128]{1,0:T(8,128)S(1)}, f32[64,128]{1,0:T(8,128)}, u32[]{:S(2)}) copy-start(f32[64,128]{1,0:T(8,128)} %constant.21.clone.cos_ref) | copy-start | bytes 98308
  1.6 30.3 %copy-start.5 = (f32[64,128]{1,0:T(8,128)S(1)}, f32[64,128]{1,0:T(8,128)}, u32[]{:S(2)}) copy-start(f32[64,128]{1,0:T(8,128)} %constant.22.clone.sin_ref) | copy-start | bytes 98308
  34.2 12.7 %copy-start.6 = (f32[192]{0:T(256)S(1)}, f32[192]{0:T(256)}, u32[]{:S(2)}) copy-start(f32[192]{0:T(256)} %param.11) | copy-start | bytes 2308
  34.2 25.7 %all-to-all-start.1 = ((f32[128,1,2304]{2,1,0:T(1,128)}), f32[128,1,2304]{2,1,0:T(1,128)S(1)}, u32[]{:S(2)}, u32[]{:S(2)}) async-start(f32[128,1,2304]{2,1,0:T(1,128)} %bitcast.3), calls=%async_computation.1 | async-start | bytes 2359296 | tf_op jit(solution)/shard_map/all_to_all | solution.py:209
  39.7 20.2 %collective-permute-start = (f32[3,1536]{1,0:T(4,128)S(1)}, f32[3,1536]{1,0:T(4,128)S(1)}, u32[]{:S(2)}, u32[]{:S(2)}) collective-permute-start(f32[3,1536]{1,0:T(4,128)S(1)} %get-tuple-element.13), channel_id=1, source_target_pairs={{0,1},{1,2},{2,3},{3,4},{4,5},{5,6},{6,7},{7,8},{8,9},{9,10},{10,1... | collective-permute-start | bytes 55304 | tf_op jit(solution)/shard_map/ppermute | solution.py:251
  39.8 20.1 %collective-permute-start.1 = (f32[3,1536]{1,0:T(4,128)S(1)}, f32[3,1536]{1,0:T(4,128)S(1)}, u32[]{:S(2)}, u32[]{:S(2)}) collective-permute-start(f32[3,1536]{1,0:T(4,128)S(1)} %get-tuple-element.14), channel_id=1, source_target_pairs={{1,0},{2,1},{3,2},{4,3},{5,4},{6,5},{7,6},{8,7},{9,8},{10,9},{11,1... | collective-permute-start | bytes 55304 | tf_op jit(solution)/shard_map/ppermute | solution.py:252

commit v4 on v3

--- a/solution.py
+++ b/solution.py
@@ -13,6 +13,7 @@
 LANES = 128
 AXES = ("y", "z", "x", "core")
 RANKS = ("core", "z", "x", "y")
+VMEM_LIMIT = 12 * 2**20
 
 
 def split_const(table):
@@ -103,7 +104,9 @@
         last_ref[c : c + 1, :] = held[c, span - 1 : span, :]
 
 
-def smooth_kernel(x_ref, f_ref, r_ref, e_ref, b_ref, cos_ref, sin_ref, out_ref, z_ref, w_ref, lone_ref):
+def smooth_kernel(
+    x_ref, f_ref, r_ref, e_ref, b_ref, cos_ref, sin_ref, _forcing, _gain, out_ref, z_ref, w_ref, lone_ref
+):
     devices = f_ref.shape[0] // 2
     half = devices // 2
     groups = x_ref.shape[0] // devices
@@ -227,27 +230,16 @@
     away = pl.BlockSpec(memory_space=pltpu.HBM)
     edge = pltpu.VMEM((comps, merged), f32)
     rows = pltpu.VMEM((devices * groups, LANES), f32)
-    v = jnp.transpose(velocity, (1, 0, 2))
+    v = pltpu.with_memory_space_constraint(jnp.transpose(velocity, (1, 0, 2)), pltpu.HBM)
     sent, first, last = pl.pallas_call(
         pack_kernel,
+        compiler_params=pltpu.CompilerParams(vmem_limit_bytes=VMEM_LIMIT),
         in_specs=[away],
         out_specs=(here,) * 3,
         out_shape=(rows, edge, edge),
         scratch_shapes=[pltpu.VMEM(v.shape, f32), pltpu.SemaphoreType.DMA((3,))],
     )(v)
     got = exchange(sent, devices)
-    smoothed = pl.pallas_call(
-        smooth_kernel,
-        in_specs=[here] * 7,
-        out_specs=here,
-        out_shape=rows,
-        scratch_shapes=[
-            pltpu.VMEM((groups * devices, LANES), f32),
-            pltpu.VMEM((devices, groups * LANES), f32),
-            pltpu.VMEM((1, groups * LANES), f32),
-        ],
-    )(in_vmem(got), *(in_vmem(jnp.asarray(t)) for t in tables(sizes, span)))
-    back = exchange(smoothed, devices)
     before = lax.ppermute(last, AXES, [(i, (i + 1) % devices) for i in range(devices)])
     after = lax.ppermute(first, AXES, [((i + 1) % devices, i) for i in range(devices)])
     padded = jnp.pad(base_flow, 1)
@@ -257,13 +249,34 @@
     place = jnp.asarray((lane[None, :] == np.arange(wall_rows)[:, None]).astype(ml_dtypes.bfloat16))
     forcing, gain = pl.pallas_call(
         functools.partial(forcing_kernel, normal=normal),
+        compiler_params=pltpu.CompilerParams(vmem_limit_bytes=VMEM_LIMIT),
         in_specs=[here] * 5,
         out_specs=(here,) * 2,
         out_shape=(pltpu.VMEM(v.shape, f32), pltpu.VMEM((2, merged), f32)),
         cost_estimate=pl.CostEstimate(flops=0, bytes_accessed=10_000_000, transcendentals=0),
     )(v, flow, slope, slot_mask, place)
+    smoothed = pl.pallas_call(
+        smooth_kernel,
+        compiler_params=pltpu.CompilerParams(vmem_limit_bytes=VMEM_LIMIT),
+        in_specs=[here] * 9,
+        out_specs=here,
+        out_shape=rows,
+        scratch_shapes=[
+            pltpu.VMEM((groups * devices, LANES), f32),
+            pltpu.VMEM((devices, groups * LANES), f32),
+            pltpu.VMEM((1, groups * LANES), f32),
+        ],
+        cost_estimate=pl.CostEstimate(flops=0, bytes_accessed=1000, transcendentals=0),
+    )(
+        in_vmem(got),
+        *(in_vmem(jnp.asarray(t)) for t in tables(sizes, span)),
+        *(in_vmem(t) for t in (forcing, gain)),
+    )
+    smoothed, before, after = lax.optimization_barrier((smoothed, before, after))
+    back = exchange(smoothed, devices)
     out = pl.pallas_call(
         unpack_kernel,
+        compiler_params=pltpu.CompilerParams(vmem_limit_bytes=VMEM_LIMIT),
         in_specs=[here] * 5,
         out_specs=away,
         out_shape=jax.ShapeDtypeStruct(v.shape, f32),

time: 61.4 us -> 60.6 us (0.987)
  blocking collectives: 30.3 us -> 24.6 us
  starting transfers between devices: 12.7 us -> 18.4 us
  local copies, waits for them, and re-layouts: 1.4 us -> 0.23 us
    all_to_all x1, waiting for transfers between devices: 0.01 us -> 8.99 us  [exchange(): lax.all_to_all(rows.reshape(devices, 1, -1), RANKS, split_axis=0, concat_...]
    ppermute x1, waiting for transfers between devices: 8.75 us -> 0.01 us  [body(): lax.ppermute(last, AXES, [(i, (i + 1) % devices) for i in range(devices)])]
    all_to_all x1, starting transfers between devices: 5.44 us -> 11.1 us  [exchange(): lax.all_to_all(rows.reshape(devices, 1, -1), RANKS, split_axis=0, concat_...]
    all_to_all x1, blocking collectives: 30.3 us -> 24.6 us  [exchange(): lax.all_to_all(rows.reshape(devices, 1, -1), RANKS, split_axis=0, concat_...]
  transfers between devices with their start and end apart: 3 -> 3, of which waited for: 1 -> 1; matrix products, arithmetic and copies ran while one was open for 2% -> 0% of each run, Pallas kernels for 5% -> 7%
where the time goes in v4:
time: 60.6 us; the launch traced here: 60.2 us
  blocking collectives  24.6 us (41%)
  starting transfers between devices  18.4 us (30%)
  waiting for transfers between devices  9 us (15%)
  Pallas kernels  7.82 us (13%)
    all_to_all x1, blocking collectives, exchange(): lax.all_to_all(rows.reshape(devices, 1, -1), RANKS, split_axis=0, concat_...  24.6 us
    all_to_all x1, starting transfers between devices, exchange(): lax.all_to_all(rows.reshape(devices, 1, -1), RANKS, split_axis=0, concat_...  11.1 us
    all_to_all x1, waiting for transfers between devices, exchange(): lax.all_to_all(rows.reshape(devices, 1, -1), RANKS, split_axis=0, concat_...  8.99 us
    ppermute x1, starting transfers between devices, body(): lax.ppermute(first, AXES, [((i + 1) % devices, i) for i in range(devices)])  7.16 us
    pallas_call x1, Pallas kernels, body(): pl.pallas_call(functools.partial(forcing_kernel, normal=normal), compiler...  2.76 us
    pallas_call x1, Pallas kernels, body(): pl.pallas_call(pack_kernel, compiler_params=pltpu.CompilerParams(vmem_lim...  2.55 us
    pallas_call x1, Pallas kernels, body(): pl.pallas_call(smooth_kernel, compiler_params=pltpu.CompilerParams(vmem_l...  1.31 us
  transfers between devices with their start and end apart: 3, of which 1 were waited for; matrix products, arithmetic and copies ran while one was open for 0% of the time, Pallas kernels for 7%

profile of v4, /device:TPU:0, one launch (start us, length us, event | category | flops | bytes accessed | tf_op | source)
XLA Modules:
  0.0 60.2 jit_solution(1504623478789286108)
XLA Ops:
  0.0 2.5 %shard_map.100 = (f32[2304,128]{1,0:T(8,128)}, f32[3,1536]{1,0:T(4,128)S(1)}, f32[3,1536]{1,0:T(4,128)S(1)}) custom-call(f32[3,64,1536]{2,1,0:T(8,128)} %bitcast.9), custom_call_target="tpu_custom_call" | custom-call | tf_op jit(solution)/shard_map/pallas_call | solution.py:234
  2.6 0.0 copy-start.8
  2.6 0.0 copy-start.6
  2.6 0.0 copy-start.7
  2.6 11.1 %all-to-all-start = ((f32[128,1,2304]{2,1,0:T(1,128)}), f32[128,1,2304]{2,1,0:T(1,128)S(1)}, u32[]{:S(2)}, u32[]{:S(2)}) async-start(f32[128,1,2304]{2,1,0:T(1,128)} %bitcast.1), calls=%async_computation | async-start | bytes 2359296 | tf_op jit(solution)/shard_map/all_to_all | solution.py:212
  13.7 0.0 copy-start
  13.8 0.0 copy-start.1
  13.8 0.0 copy-start.2
  13.8 0.0 copy-start.3
  13.8 0.0 copy-start.4
  13.8 0.0 copy-start.5
  13.8 0.1 collective-permute-start
  13.9 7.2 %collective-permute-start.1 = (f32[3,1536]{1,0:T(4,128)S(1)}, f32[3,1536]{1,0:T(4,128)S(1)}, u32[]{:S(2)}, u32[]{:S(2)}) collective-permute-start(f32[3,1536]{1,0:T(4,128)S(1)} %get-tuple-element.17), channel_id=1, source_target_pairs={{1,0},{2,1},{3,2},{4,3},{5,4},{6,5},{7,6},{8,7},{9,8},{10,9},{11,1... | collective-permute-start | bytes 55304 | tf_op jit(solution)/shard_map/ppermute | solution.py:244
  21.1 0.0 copy-done.8
  21.1 0.1 slice_subtract_fusion
  21.2 0.1 broadcast_in_dim_tile.7.slope_ref
  21.2 0.1 broadcast_in_dim_tile.6.flow_ref
  21.3 0.0 copy-done.6
  21.3 0.0 copy-done.7
  21.3 2.8 %shard_map.101 = (f32[3,64,1536]{2,1,0:T(8,128)S(1)}, f32[2,1536]{1,0:T(2,128)S(1)}) custom-call(f32[3,64,1536]{2,1,0:T(8,128)} %bitcast.10, f32[1,1536]{1,0:T(1,128)S(1)} %broadcast_in_dim_tile.6.flow_ref, f32[1,1536]{1,0:T(1,128)S(1)} %broadcast_in_dim_tile.7.slope_ref, s32[8,64]{1,0:T(8,128)S(1)} %copy-done.7, bf16[8,1536]{1,0:T(8,128)(2,1)S(1)} %copy-done.6), custom_call_target="tpu_custom_call" | custom-call | bytes 10000000 | tf_op jit(solution)/shard_map/pallas_call | solution.py:250
  24.1 9.0 %all-to-all-done = f32[128,1,2304]{2,1,0:T(1,128)S(1)} async-done(((f32[128,1,2304]{2,1,0:T(1,128)}), f32[128,1,2304]{2,1,0:T(1,128)S(1)}, u32[]{:S(2)}, u32[]{:S(2)}) %all-to-all-start) | async-done | bytes 1179680 | tf_op jit(solution)/shard_map/all_to_all | solution.py:212
  33.1 0.0 copy-done
  33.1 0.0 copy-done.1
  33.1 0.0 copy-done.2
  33.1 0.0 copy-done.3
  33.1 0.0 copy-done.4
  33.1 0.0 copy-done.5
  33.1 1.3 %shard_map.102 = f32[2304,128]{1,0:T(8,128)S(1)} custom-call(f32[2304,128]{1,0:T(8,128)S(1)} %bitcast.6, bf16[256,256]{1,0:T(8,128)(2,1)S(1)} %copy-done.3, bf16[256,256]{1,0:T(8,128)(2,1)S(1)} %copy-done.2, bf16[256,256]{1,0:T(8,128)(2,1)S(1)} %copy-done.1, bf16[256,256]{1,0:T(8,128)(2,1)S(1)} %copy-done, f32[64,128]{1,0:T(8,128)S(1)} %copy-done.5, ...), custom_call_target="tpu_custom_call" | custom-call | bytes 1000 | tf_op jit(solution)/shard_map/pallas_call | solution.py:258
  34.4 0.0 collective-permute-done.before_ref
  34.5 0.0 collective-permute-done.1.after_ref
  34.5 24.6 %all_to_all.10 = f32[128,1,2304]{2,1,0:T(1,128)S(1)} all-to-all(f32[128,1,2304]{2,1,0:T(1,128)S(1)} %bitcast.7), channel_id=1, replica_groups=mesh['y'=4,'z'=4,'x'=4,'core'=2] {'core','z','x','y'}, dimensions={0} | all-to-all | bytes 2359296 | tf_op jit(solution)/shard_map/all_to_all | solution.py:212
  59.0 1.2 %shard_map.103 = f32[3,64,1536]{2,1,0:T(8,128)} custom-call(f32[2304,128]{1,0:T(8,128)S(1)} %bitcast.8, f32[3,64,1536]{2,1,0:T(8,128)S(1)} %get-tuple-element.14._forcing.f_ref, f32[2,1536]{1,0:T(2,128)S(1)} %get-tuple-element.15._gain.gain_ref, f32[3,1536]{1,0:T(4,128)S(1)} %collective-permute-done.before_ref, f32[3,1536]{1,0:T(4,128)S(1)} %collective-permute-done.1.after_ref), custom_call_target="tpu_custom_call" | custom-call | tf_op jit(solution)/shard_map/pallas_call | solution.py:277
  (2 shorter events, 0.0 us)
Async XLA Ops:
  2.6 18.5 %copy-start.8 = (f32[192]{0:T(256)S(1)}, f32[192]{0:T(256)}, u32[]{:S(2)}) copy-start(f32[192]{0:T(256)} %param.11) | copy-start | bytes 2308
  2.6 18.8 %copy-start.6 = (bf16[8,1536]{1,0:T(8,128)(2,1)S(1)}, bf16[8,1536]{1,0:T(8,128)(2,1)}, u32[]{:S(2)}) copy-start(bf16[8,1536]{1,0:T(8,128)(2,1)} %constant.17.clone.place_ref) | copy-start | bytes 73732
  2.6 18.7 %copy-start.7 = (s32[8,64]{1,0:T(8,128)S(1)}, s32[8,64]{1,0:T(8,128)}, u32[]{:S(2)}) copy-start(s32[8,64]{1,0:T(8,128)} %mask_ref.1) | copy-start | bytes 6148
  2.6 30.5 %all-to-all-start = ((f32[128,1,2304]{2,1,0:T(1,128)}), f32[128,1,2304]{2,1,0:T(1,128)S(1)}, u32[]{:S(2)}, u32[]{:S(2)}) async-start(f32[128,1,2304]{2,1,0:T(1,128)} %bitcast.1), calls=%async_computation | async-start | bytes 2359296 | tf_op jit(solution)/shard_map/all_to_all | solution.py:212
  13.7 19.3 %copy-start = (bf16[256,256]{1,0:T(8,128)(2,1)S(1)}, bf16[256,256]{1,0:T(8,128)(2,1)}, u32[]{:S(2)}) copy-start(bf16[256,256]{1,0:T(8,128)(2,1)} %constant.21.clone.b_ref) | copy-start | bytes 393220
  13.8 19.3 %copy-start.1 = (bf16[256,256]{1,0:T(8,128)(2,1)S(1)}, bf16[256,256]{1,0:T(8,128)(2,1)}, u32[]{:S(2)}) copy-start(bf16[256,256]{1,0:T(8,128)(2,1)} %constant.20.clone.e_ref) | copy-start | bytes 393220
  13.8 19.3 %copy-start.2 = (bf16[256,256]{1,0:T(8,128)(2,1)S(1)}, bf16[256,256]{1,0:T(8,128)(2,1)}, u32[]{:S(2)}) copy-start(bf16[256,256]{1,0:T(8,128)(2,1)} %constant.19.clone.r_ref) | copy-start | bytes 393220
  13.8 19.3 %copy-start.3 = (bf16[256,256]{1,0:T(8,128)(2,1)S(1)}, bf16[256,256]{1,0:T(8,128)(2,1)}, u32[]{:S(2)}) copy-start(bf16[256,256]{1,0:T(8,128)(2,1)} %constant.18.clone.f_ref) | copy-start | bytes 393220
  13.8 19.3 %copy-start.4 = (f32[64,128]{1,0:T(8,128)S(1)}, f32[64,128]{1,0:T(8,128)}, u32[]{:S(2)}) copy-start(f32[64,128]{1,0:T(8,128)} %constant.23.clone.sin_ref) | copy-start | bytes 98308
  13.8 19.3 %copy-start.5 = (f32[64,128]{1,0:T(8,128)S(1)}, f32[64,128]{1,0:T(8,128)}, u32[]{:S(2)}) copy-start(f32[64,128]{1,0:T(8,128)} %constant.22.clone.cos_ref) | copy-start | bytes 98308
  13.8 20.6 %collective-permute-start = (f32[3,1536]{1,0:T(4,128)S(1)}, f32[3,1536]{1,0:T(4,128)S(1)}, u32[]{:S(2)}, u32[]{:S(2)}) collective-permute-start(f32[3,1536]{1,0:T(4,128)S(1)} %get-tuple-element.16), channel_id=1, source_target_pairs={{0,1},{1,2},{2,3},{3,4},{4,5},{5,6},{6,7},{7,8},{8,9},{9,10},{10,1... | collective-permute-start | bytes 55304 | tf_op jit(solution)/shard_map/ppermute | solution.py:243
  13.9 20.6 %collective-permute-start.1 = (f32[3,1536]{1,0:T(4,128)S(1)}, f32[3,1536]{1,0:T(4,128)S(1)}, u32[]{:S(2)}, u32[]{:S(2)}) collective-permute-start(f32[3,1536]{1,0:T(4,128)S(1)} %get-tuple-element.17), channel_id=1, source_target_pairs={{1,0},{2,1},{3,2},{4,3},{5,4},{6,5},{7,6},{8,7},{9,8},{10,9},{11,1... | collective-permute-start | bytes 55304 | tf_op jit(solution)/shard_map/ppermute | solution.py:244

commit v5 on v4

--- a/solution.py
+++ b/solution.py
@@ -111,11 +111,13 @@
     half = devices // 2
     groups = x_ref.shape[0] // devices
 
+    block = math.gcd(groups, 6)
+
     def outer(p):
         cos, sin = cos_ref[...], sin_ref[...]
-        pair = [x_ref[pl.ds(p + i, devices, stride=groups), :] for i in range(2)]
-        y = dot_rows(f_ref[...], jnp.concatenate(pair, axis=1))
-        for i in range(2):
+        lines = [x_ref[pl.ds(p + i, devices, stride=groups), :] for i in range(block)]
+        y = dot_rows(f_ref[...], jnp.concatenate(lines, axis=1))
+        for i in range(block):
             at = (p + i) * devices
             re = y[:half, i * LANES : (i + 1) * LANES]
             im = y[half:, i * LANES : (i + 1) * LANES]
@@ -124,8 +126,8 @@
 
     def inner(p):
         cos, sin = cos_ref[...], sin_ref[...]
-        w = dot_lanes(z_ref[p * devices : (p + 2) * devices, :], r_ref[...])
-        for i in range(2):
+        w = dot_lanes(z_ref[p * devices : (p + block) * devices, :], r_ref[...])
+        for i in range(block):
             at = (p + i) * LANES
             re = w[i * devices : i * devices + half]
             im = w[i * devices + half : (i + 1) * devices]
@@ -140,18 +142,18 @@
             lone_ref[:, p * LANES : (p + 1) * LANES] = lone[p : p + 1]
 
     def outer_back(p):
-        both = slice(p * LANES, (p + 2) * LANES)
-        y = dot_rows(b_ref[...], w_ref[:, both]) + lone_ref[:, both]
-        for i in range(2):
+        lines = slice(p * LANES, (p + block) * LANES)
+        y = dot_rows(b_ref[...], w_ref[:, lines]) + lone_ref[:, lines]
+        for i in range(block):
             out_ref[pl.ds(p + i, devices, stride=groups), :] = y[:, i * LANES : (i + 1) * LANES]
 
-    for p in range(0, groups + 2, 2):
+    for p in range(0, groups + block, block):
         if p < groups:
             outer(p)
-        if p >= 2:
-            inner(p - 2)
+        if p >= block:
+            inner(p - block)
     extra()
-    for p in range(0, groups, 2):
+    for p in range(0, groups, block):
         outer_back(p)
 
 
@@ -192,18 +194,25 @@
     comps, span, merged = f_ref.shape
     pairs = merged // (2 * LANES)
     groups = s_ref.shape[0] // LANES
+    parts = sems.shape[0] // comps
+    width = merged // parts
     stores = []
     for c in range(comps):
-        for q in range(pairs):
-            both = s_ref[pl.ds(c * pairs + q, LANES, stride=groups), :].T
-            lo = slice(q * 2 * LANES, q * 2 * LANES + LANES)
-            hi = slice(q * 2 * LANES + LANES, (q + 1) * 2 * LANES)
-            held[c, :, lo] = f_ref[c, :, lo] + both[:span]
-            held[c, :, hi] = f_ref[c, :, hi] + both[span:]
-        held[c, 0:1, :] = held[c, 0:1, :] + gain_ref[0:1, :] * before_ref[c : c + 1, :]
-        held[c, span - 1 : span, :] = held[c, span - 1 : span, :] + gain_ref[1:2, :] * after_ref[c : c + 1, :]
-        stores.append(pltpu.make_async_copy(held.at[c], out_ref.at[c], sems.at[c]))
-        stores[-1].start()
+        for h in range(parts):
+            for q in range(h * pairs // parts, (h + 1) * pairs // parts):
+                both = s_ref[pl.ds(c * pairs + q, LANES, stride=groups), :].T
+                lo = slice(q * 2 * LANES, q * 2 * LANES + LANES)
+                hi = slice(q * 2 * LANES + LANES, (q + 1) * 2 * LANES)
+                held[c, :, lo] = f_ref[c, :, lo] + both[:span]
+                held[c, :, hi] = f_ref[c, :, hi] + both[span:]
+            part = slice(h * width, (h + 1) * width)
+            low = gain_ref[0:1, part] * before_ref[c : c + 1, part]
+            high = gain_ref[1:2, part] * after_ref[c : c + 1, part]
+            held[c, 0:1, part] = held[c, 0:1, part] + low
+            held[c, span - 1 : span, part] = held[c, span - 1 : span, part] + high
+            piece = (c, slice(None), pl.ds(h * width, width))
+            stores.append(pltpu.make_async_copy(held.at[piece], out_ref.at[piece], sems.at[c * parts + h]))
+            stores[-1].start()
     for store in stores:
         store.wait()
 
@@ -280,7 +289,7 @@
         in_specs=[here] * 5,
         out_specs=away,
         out_shape=jax.ShapeDtypeStruct(v.shape, f32),
-        scratch_shapes=[pltpu.VMEM(v.shape, f32), pltpu.SemaphoreType.DMA((comps,))],
+        scratch_shapes=[pltpu.VMEM(v.shape, f32), pltpu.SemaphoreType.DMA((2 * comps,))],
     )(in_vmem(back), in_vmem(forcing), in_vmem(gain), in_vmem(before), in_vmem(after))
     return jnp.transpose(out, (1, 0, 2))
 

time: 60.6 us -> 60.5 us (level)
  no operation moved by 1% of the time
where the time goes in v5:
time: 60.5 us; the launch traced here: 60.1 us
  blocking collectives  24.6 us (41%)
  starting transfers between devices  18.4 us (30%)
  waiting for transfers between devices  9 us (15%)
  Pallas kernels  7.7 us (13%)
    all_to_all x1, blocking collectives, exchange(): lax.all_to_all(rows.reshape(devices, 1, -1), RANKS, split_axis=0, concat_...  24.6 us
    all_to_all x1, starting transfers between devices, exchange(): lax.all_to_all(rows.reshape(devices, 1, -1), RANKS, split_axis=0, concat_...  11.1 us
    all_to_all x1, waiting for transfers between devices, exchange(): lax.all_to_all(rows.reshape(devices, 1, -1), RANKS, split_axis=0, concat_...  8.99 us
    ppermute x1, starting transfers between devices, body(): lax.ppermute(first, AXES, [((i + 1) % devices, i) for i in range(devices)])  7.16 us
    pallas_call x1, Pallas kernels, body(): pl.pallas_call(functools.partial(forcing_kernel, normal=normal), compiler...  2.76 us
    pallas_call x1, Pallas kernels, body(): pl.pallas_call(pack_kernel, compiler_params=pltpu.CompilerParams(vmem_lim...  2.55 us
  transfers between devices with their start and end apart: 3, of which 1 were waited for; matrix products, arithmetic and copies ran while one was open for 0% of the time, Pallas kernels for 7%

profile of v5, /device:TPU:0, one launch (start us, length us, event | category | flops | bytes accessed | tf_op | source)
XLA Modules:
  0.0 60.1 jit_solution(2820583472455198886)
XLA Ops:
  0.0 2.5 %shard_map.100 = (f32[2304,128]{1,0:T(8,128)}, f32[3,1536]{1,0:T(4,128)S(1)}, f32[3,1536]{1,0:T(4,128)S(1)}) custom-call(f32[3,64,1536]{2,1,0:T(8,128)} %bitcast.9), custom_call_target="tpu_custom_call" | custom-call | tf_op jit(solution)/shard_map/pallas_call | solution.py:243
  2.6 0.0 copy-start.8
  2.6 0.0 copy-start.6
  2.6 0.0 copy-start.7
  2.6 11.1 %all-to-all-start = ((f32[128,1,2304]{2,1,0:T(1,128)}), f32[128,1,2304]{2,1,0:T(1,128)S(1)}, u32[]{:S(2)}, u32[]{:S(2)}) async-start(f32[128,1,2304]{2,1,0:T(1,128)} %bitcast.1), calls=%async_computation | async-start | bytes 2359296 | tf_op jit(solution)/shard_map/all_to_all | solution.py:221
  13.7 0.0 copy-start
  13.8 0.0 copy-start.1
  13.8 0.0 copy-start.2
  13.8 0.0 copy-start.3
  13.8 0.0 copy-start.4
  13.8 0.0 copy-start.5
  13.8 0.1 collective-permute-start
  13.9 7.2 %collective-permute-start.1 = (f32[3,1536]{1,0:T(4,128)S(1)}, f32[3,1536]{1,0:T(4,128)S(1)}, u32[]{:S(2)}, u32[]{:S(2)}) collective-permute-start(f32[3,1536]{1,0:T(4,128)S(1)} %get-tuple-element.17), channel_id=1, source_target_pairs={{1,0},{2,1},{3,2},{4,3},{5,4},{6,5},{7,6},{8,7},{9,8},{10,9},{11,1... | collective-permute-start | bytes 55304 | tf_op jit(solution)/shard_map/ppermute | solution.py:253
  21.1 0.0 copy-done.8
  21.1 0.1 slice_subtract_fusion
  21.2 0.1 broadcast_in_dim_tile.7.slope_ref
  21.2 0.1 broadcast_in_dim_tile.6.flow_ref
  21.3 0.0 copy-done.6
  21.3 0.0 copy-done.7
  21.3 2.8 %shard_map.101 = (f32[3,64,1536]{2,1,0:T(8,128)S(1)}, f32[2,1536]{1,0:T(2,128)S(1)}) custom-call(f32[3,64,1536]{2,1,0:T(8,128)} %bitcast.10, f32[1,1536]{1,0:T(1,128)S(1)} %broadcast_in_dim_tile.6.flow_ref, f32[1,1536]{1,0:T(1,128)S(1)} %broadcast_in_dim_tile.7.slope_ref, s32[8,64]{1,0:T(8,128)S(1)} %copy-done.7, bf16[8,1536]{1,0:T(8,128)(2,1)S(1)} %copy-done.6), custom_call_target="tpu_custom_call" | custom-call | bytes 10000000 | tf_op jit(solution)/shard_map/pallas_call | solution.py:259
  24.1 9.0 %all-to-all-done = f32[128,1,2304]{2,1,0:T(1,128)S(1)} async-done(((f32[128,1,2304]{2,1,0:T(1,128)}), f32[128,1,2304]{2,1,0:T(1,128)S(1)}, u32[]{:S(2)}, u32[]{:S(2)}) %all-to-all-start) | async-done | bytes 1179680 | tf_op jit(solution)/shard_map/all_to_all | solution.py:221
  33.1 0.0 copy-done
  33.1 0.0 copy-done.1
  33.1 0.0 copy-done.2
  33.1 0.0 copy-done.3
  33.1 0.0 copy-done.4
  33.1 0.0 copy-done.5
  33.1 1.2 %shard_map.102 = f32[2304,128]{1,0:T(8,128)S(1)} custom-call(f32[2304,128]{1,0:T(8,128)S(1)} %bitcast.6, bf16[256,256]{1,0:T(8,128)(2,1)S(1)} %copy-done.3, bf16[256,256]{1,0:T(8,128)(2,1)S(1)} %copy-done.2, bf16[256,256]{1,0:T(8,128)(2,1)S(1)} %copy-done.1, bf16[256,256]{1,0:T(8,128)(2,1)S(1)} %copy-done, f32[64,128]{1,0:T(8,128)S(1)} %copy-done.5, ...), custom_call_target="tpu_custom_call" | custom-call | bytes 1000 | tf_op jit(solution)/shard_map/pallas_call | solution.py:267
  34.3 0.0 collective-permute-done.before_ref
  34.4 0.0 collective-permute-done.1.after_ref
  34.4 24.6 %all_to_all.10 = f32[128,1,2304]{2,1,0:T(1,128)S(1)} all-to-all(f32[128,1,2304]{2,1,0:T(1,128)S(1)} %bitcast.7), channel_id=1, replica_groups=mesh['y'=4,'z'=4,'x'=4,'core'=2] {'core','z','x','y'}, dimensions={0} | all-to-all | bytes 2359296 | tf_op jit(solution)/shard_map/all_to_all | solution.py:221
  58.9 1.2 %shard_map.103 = f32[3,64,1536]{2,1,0:T(8,128)} custom-call(f32[2304,128]{1,0:T(8,128)S(1)} %bitcast.8, f32[3,64,1536]{2,1,0:T(8,128)S(1)} %get-tuple-element.14._forcing.f_ref, f32[2,1536]{1,0:T(2,128)S(1)} %get-tuple-element.15._gain.gain_ref, f32[3,1536]{1,0:T(4,128)S(1)} %collective-permute-done.before_ref, f32[3,1536]{1,0:T(4,128)S(1)} %collective-permute-done.1.after_ref), custom_call_target="tpu_custom_call" | custom-call | tf_op jit(solution)/shard_map/pallas_call | solution.py:286
  (2 shorter events, 0.0 us)
Async XLA Ops:
  2.6 18.5 %copy-start.8 = (f32[192]{0:T(256)S(1)}, f32[192]{0:T(256)}, u32[]{:S(2)}) copy-start(f32[192]{0:T(256)} %param.11) | copy-start | bytes 2308
  2.6 18.8 %copy-start.6 = (bf16[8,1536]{1,0:T(8,128)(2,1)S(1)}, bf16[8,1536]{1,0:T(8,128)(2,1)}, u32[]{:S(2)}) copy-start(bf16[8,1536]{1,0:T(8,128)(2,1)} %constant.17.clone.place_ref) | copy-start | bytes 73732
  2.6 18.7 %copy-start.7 = (s32[8,64]{1,0:T(8,128)S(1)}, s32[8,64]{1,0:T(8,128)}, u32[]{:S(2)}) copy-start(s32[8,64]{1,0:T(8,128)} %mask_ref.1) | copy-start | bytes 6148
  2.6 30.5 %all-to-all-start = ((f32[128,1,2304]{2,1,0:T(1,128)}), f32[128,1,2304]{2,1,0:T(1,128)S(1)}, u32[]{:S(2)}, u32[]{:S(2)}) async-start(f32[128,1,2304]{2,1,0:T(1,128)} %bitcast.1), calls=%async_computation | async-start | bytes 2359296 | tf_op jit(solution)/shard_map/all_to_all | solution.py:221
  13.7 19.3 %copy-start = (bf16[256,256]{1,0:T(8,128)(2,1)S(1)}, bf16[256,256]{1,0:T(8,128)(2,1)}, u32[]{:S(2)}) copy-start(bf16[256,256]{1,0:T(8,128)(2,1)} %constant.21.clone.b_ref) | copy-start | bytes 393220
  13.8 19.3 %copy-start.1 = (bf16[256,256]{1,0:T(8,128)(2,1)S(1)}, bf16[256,256]{1,0:T(8,128)(2,1)}, u32[]{:S(2)}) copy-start(bf16[256,256]{1,0:T(8,128)(2,1)} %constant.20.clone.e_ref) | copy-start | bytes 393220
  13.8 19.3 %copy-start.2 = (bf16[256,256]{1,0:T(8,128)(2,1)S(1)}, bf16[256,256]{1,0:T(8,128)(2,1)}, u32[]{:S(2)}) copy-start(bf16[256,256]{1,0:T(8,128)(2,1)} %constant.19.clone.r_ref) | copy-start | bytes 393220
  13.8 19.3 %copy-start.3 = (bf16[256,256]{1,0:T(8,128)(2,1)S(1)}, bf16[256,256]{1,0:T(8,128)(2,1)}, u32[]{:S(2)}) copy-start(bf16[256,256]{1,0:T(8,128)(2,1)} %constant.18.clone.f_ref) | copy-start | bytes 393220
  13.8 19.3 %copy-start.4 = (f32[64,128]{1,0:T(8,128)S(1)}, f32[64,128]{1,0:T(8,128)}, u32[]{:S(2)}) copy-start(f32[64,128]{1,0:T(8,128)} %constant.23.clone.sin_ref) | copy-start | bytes 98308
  13.8 19.3 %copy-start.5 = (f32[64,128]{1,0:T(8,128)S(1)}, f32[64,128]{1,0:T(8,128)}, u32[]{:S(2)}) copy-start(f32[64,128]{1,0:T(8,128)} %constant.22.clone.cos_ref) | copy-start | bytes 98308
  13.8 20.5 %collective-permute-start = (f32[3,1536]{1,0:T(4,128)S(1)}, f32[3,1536]{1,0:T(4,128)S(1)}, u32[]{:S(2)}, u32[]{:S(2)}) collective-permute-start(f32[3,1536]{1,0:T(4,128)S(1)} %get-tuple-element.16), channel_id=1, source_target_pairs={{0,1},{1,2},{2,3},{3,4},{4,5},{5,6},{6,7},{7,8},{8,9},{9,10},{10,1... | collective-permute-start | bytes 55304 | tf_op jit(solution)/shard_map/ppermute | solution.py:252
  13.9 20.4 %collective-permute-start.1 = (f32[3,1536]{1,0:T(4,128)S(1)}, f32[3,1536]{1,0:T(4,128)S(1)}, u32[]{:S(2)}, u32[]{:S(2)}) collective-permute-start(f32[3,1536]{1,0:T(4,128)S(1)} %get-tuple-element.17), channel_id=1, source_target_pairs={{1,0},{2,1},{3,2},{4,3},{5,4},{6,5},{7,6},{8,7},{9,8},{10,9},{11,1... | collective-permute-start | bytes 55304 | tf_op jit(solution)/shard_map/ppermute | solution.py:253

commit v6 on v5

--- a/solution.py
+++ b/solution.py
@@ -81,27 +81,36 @@
     return both[:, :lanes] + both[:, lanes:]
 
 
-def pack_kernel(v_ref, out_ref, first_ref, last_ref, held, sems):
+def pack_kernel(v_ref, out_ref, first_ref, last_ref, held, turned, load_sems, store_sems):
     comps, span, merged = v_ref.shape
     pairs = merged // (2 * LANES)
     groups = out_ref.shape[0] // LANES
-    steps = sems.shape[0]
+    steps = load_sems.shape[0]
     width = merged // steps
     loads = []
     for i in range(steps):
         piece = (slice(None), slice(None), pl.ds(i * width, width))
-        loads.append(pltpu.make_async_copy(v_ref.at[piece], held.at[piece], sems.at[i]))
+        loads.append(pltpu.make_async_copy(v_ref.at[piece], held.at[piece], load_sems.at[i]))
         loads[-1].start()
+    stores = []
+    by_device = (LANES, groups, LANES)
     for i in range(steps):
         loads[i].wait()
-        for q in range(i * pairs // steps, (i + 1) * pairs // steps):
+        low, high = i * pairs // steps, (i + 1) * pairs // steps
+        for q in range(low, high):
             at = q * 2 * LANES
             for c in range(comps):
                 both = jnp.concatenate([held[c, :, at : at + LANES], held[c, :, at + LANES : at + 2 * LANES]], axis=0)
-                out_ref[pl.ds(c * pairs + q, LANES, stride=groups), :] = both.T
+                turned[pl.ds(q * comps + c, LANES, stride=groups), :] = both.T
+        piece = (slice(None), pl.ds(low * comps, (high - low) * comps), slice(None))
+        source, target = turned.reshape(by_device).at[piece], out_ref.reshape(by_device).at[piece]
+        stores.append(pltpu.make_async_copy(source, target, store_sems.at[i]))
+        stores[-1].start()
     for c in range(comps):
         first_ref[c : c + 1, :] = held[c, 0:1, :]
         last_ref[c : c + 1, :] = held[c, span - 1 : span, :]
+    for store in stores:
+        store.wait()
 
 
 def smooth_kernel(
@@ -200,7 +209,7 @@
     for c in range(comps):
         for h in range(parts):
             for q in range(h * pairs // parts, (h + 1) * pairs // parts):
-                both = s_ref[pl.ds(c * pairs + q, LANES, stride=groups), :].T
+                both = s_ref[pl.ds(q * comps + c, LANES, stride=groups), :].T
                 lo = slice(q * 2 * LANES, q * 2 * LANES + LANES)
                 hi = slice(q * 2 * LANES + LANES, (q + 1) * 2 * LANES)
                 held[c, :, lo] = f_ref[c, :, lo] + both[:span]
@@ -244,9 +253,14 @@
         pack_kernel,
         compiler_params=pltpu.CompilerParams(vmem_limit_bytes=VMEM_LIMIT),
         in_specs=[away],
-        out_specs=(here,) * 3,
-        out_shape=(rows, edge, edge),
-        scratch_shapes=[pltpu.VMEM(v.shape, f32), pltpu.SemaphoreType.DMA((3,))],
+        out_specs=(away, here, here),
+        out_shape=(pltpu.HBM(rows.shape, f32), edge, edge),
+        scratch_shapes=[
+            pltpu.VMEM(v.shape, f32),
+            rows,
+            pltpu.SemaphoreType.DMA((3,)),
+            pltpu.SemaphoreType.DMA((3,)),
+        ],
     )(v)
     got = exchange(sent, devices)
     before = lax.ppermute(last, AXES, [(i, (i + 1) % devices) for i in range(devices)])

time: 60.5 us -> 60.2 us (level)
  no operation moved by 1% of the time
where the time goes in v6:
time: 60.2 us; the launch traced here: 59.9 us
  blocking collectives  24.6 us (41%)
  starting transfers between devices  18.4 us (31%)
  waiting for transfers between devices  9 us (15%)
  Pallas kernels  7.45 us (12%)
    all_to_all x1, blocking collectives, exchange(): lax.all_to_all(rows.reshape(devices, 1, -1), RANKS, split_axis=0, concat_...  24.6 us
    all_to_all x1, starting transfers between devices, exchange(): lax.all_to_all(rows.reshape(devices, 1, -1), RANKS, split_axis=0, concat_...  11.1 us
    all_to_all x1, waiting for transfers between devices, exchange(): lax.all_to_all(rows.reshape(devices, 1, -1), RANKS, split_axis=0, concat_...  9 us
    ppermute x1, starting transfers between devices, body(): lax.ppermute(first, AXES, [((i + 1) % devices, i) for i in range(devices)])  7.16 us
    pallas_call x1, Pallas kernels, body(): pl.pallas_call(functools.partial(forcing_kernel, normal=normal), compiler...  2.76 us
    pallas_call x1, Pallas kernels, body(): pl.pallas_call(pack_kernel, compiler_params=pltpu.CompilerParams(vmem_lim...  2.31 us
  transfers between devices with their start and end apart: 3, of which 1 were waited for; matrix products, arithmetic and copies ran while one was open for 0% of the time, Pallas kernels for 7%

profile of v6, /device:TPU:0, one launch (start us, length us, event | category | flops | bytes accessed | tf_op | source)
XLA Modules:
  0.0 59.9 jit_solution(2420274134931235195)
XLA Ops:
  0.0 2.3 %shard_map.100 = (f32[2304,128]{1,0:T(8,128)}, f32[3,1536]{1,0:T(4,128)S(1)}, f32[3,1536]{1,0:T(4,128)S(1)}) custom-call(f32[3,64,1536]{2,1,0:T(8,128)} %bitcast.9), custom_call_target="tpu_custom_call" | custom-call | tf_op jit(solution)/shard_map/pallas_call | solution.py:252
  2.3 0.0 copy-start.8
  2.3 0.0 copy-start.6
  2.3 0.0 copy-start.7
  2.4 11.1 %all-to-all-start = ((f32[128,1,2304]{2,1,0:T(1,128)}), f32[128,1,2304]{2,1,0:T(1,128)S(1)}, u32[]{:S(2)}, u32[]{:S(2)}) async-start(f32[128,1,2304]{2,1,0:T(1,128)} %bitcast.11), calls=%async_computation | async-start | bytes 2359296 | tf_op jit(solution)/shard_map/all_to_all | solution.py:230
  13.5 0.0 copy-start
  13.5 0.0 copy-start.1
  13.5 0.0 copy-start.2
  13.5 0.0 copy-start.3
  13.6 0.0 copy-start.4
  13.6 0.0 copy-start.5
  13.6 0.1 collective-permute-start
  13.7 7.2 %collective-permute-start.1 = (f32[3,1536]{1,0:T(4,128)S(1)}, f32[3,1536]{1,0:T(4,128)S(1)}, u32[]{:S(2)}, u32[]{:S(2)}) collective-permute-start(f32[3,1536]{1,0:T(4,128)S(1)} %get-tuple-element.17), channel_id=1, source_target_pairs={{1,0},{2,1},{3,2},{4,3},{5,4},{6,5},{7,6},{8,7},{9,8},{10,9},{11,1... | collective-permute-start | bytes 55304 | tf_op jit(solution)/shard_map/ppermute | solution.py:267
  20.8 0.0 copy-done.8
  20.8 0.1 slice_subtract_fusion
  20.9 0.1 broadcast_in_dim_tile.7.slope_ref
  21.0 0.1 broadcast_in_dim_tile.6.flow_ref
  21.1 0.0 copy-done.6
  21.1 0.0 copy-done.7
  21.1 2.8 %shard_map.101 = (f32[3,64,1536]{2,1,0:T(8,128)S(1)}, f32[2,1536]{1,0:T(2,128)S(1)}) custom-call(f32[3,64,1536]{2,1,0:T(8,128)} %bitcast.10, f32[1,1536]{1,0:T(1,128)S(1)} %broadcast_in_dim_tile.6.flow_ref, f32[1,1536]{1,0:T(1,128)S(1)} %broadcast_in_dim_tile.7.slope_ref, s32[8,64]{1,0:T(8,128)S(1)} %copy-done.7, bf16[8,1536]{1,0:T(8,128)(2,1)S(1)} %copy-done.6), custom_call_target="tpu_custom_call" | custom-call | bytes 10000000 | tf_op jit(solution)/shard_map/pallas_call | solution.py:273
  23.9 9.0 %all-to-all-done = f32[128,1,2304]{2,1,0:T(1,128)S(1)} async-done(((f32[128,1,2304]{2,1,0:T(1,128)}), f32[128,1,2304]{2,1,0:T(1,128)S(1)}, u32[]{:S(2)}, u32[]{:S(2)}) %all-to-all-start) | async-done | bytes 1179680 | tf_op jit(solution)/shard_map/all_to_all | solution.py:230
  32.9 0.0 copy-done
  32.9 0.0 copy-done.1
  32.9 0.0 copy-done.2
  32.9 0.0 copy-done.3
  32.9 0.0 copy-done.4
  32.9 0.0 copy-done.5
  32.9 1.2 %shard_map.102 = f32[2304,128]{1,0:T(8,128)S(1)} custom-call(f32[2304,128]{1,0:T(8,128)S(1)} %bitcast.6, bf16[256,256]{1,0:T(8,128)(2,1)S(1)} %copy-done.3, bf16[256,256]{1,0:T(8,128)(2,1)S(1)} %copy-done.2, bf16[256,256]{1,0:T(8,128)(2,1)S(1)} %copy-done.1, bf16[256,256]{1,0:T(8,128)(2,1)S(1)} %copy-done, f32[64,128]{1,0:T(8,128)S(1)} %copy-done.5, ...), custom_call_target="tpu_custom_call" | custom-call | bytes 1000 | tf_op jit(solution)/shard_map/pallas_call | solution.py:281
  34.1 0.0 collective-permute-done.before_ref
  34.1 0.0 collective-permute-done.1.after_ref
  34.1 24.6 %all_to_all.10 = f32[128,1,2304]{2,1,0:T(1,128)S(1)} all-to-all(f32[128,1,2304]{2,1,0:T(1,128)S(1)} %bitcast.7), channel_id=1, replica_groups=mesh['y'=4,'z'=4,'x'=4,'core'=2] {'core','z','x','y'}, dimensions={0} | all-to-all | bytes 2359296 | tf_op jit(solution)/shard_map/all_to_all | solution.py:230
  58.7 1.2 %shard_map.103 = f32[3,64,1536]{2,1,0:T(8,128)} custom-call(f32[2304,128]{1,0:T(8,128)S(1)} %bitcast.8, f32[3,64,1536]{2,1,0:T(8,128)S(1)} %get-tuple-element.14._forcing.f_ref, f32[2,1536]{1,0:T(2,128)S(1)} %get-tuple-element.15._gain.gain_ref, f32[3,1536]{1,0:T(4,128)S(1)} %collective-permute-done.before_ref, f32[3,1536]{1,0:T(4,128)S(1)} %collective-permute-done.1.after_ref), custom_call_target="tpu_custom_call" | custom-call | tf_op jit(solution)/shard_map/pallas_call | solution.py:300
  (2 shorter events, 0.0 us)
Async XLA Ops:
  2.3 18.5 %copy-start.8 = (f32[192]{0:T(256)S(1)}, f32[192]{0:T(256)}, u32[]{:S(2)}) copy-start(f32[192]{0:T(256)} %param.11) | copy-start | bytes 2308
  2.3 18.8 %copy-start.6 = (bf16[8,1536]{1,0:T(8,128)(2,1)S(1)}, bf16[8,1536]{1,0:T(8,128)(2,1)}, u32[]{:S(2)}) copy-start(bf16[8,1536]{1,0:T(8,128)(2,1)} %constant.17.clone.place_ref) | copy-start | bytes 73732
  2.3 18.7 %copy-start.7 = (s32[8,64]{1,0:T(8,128)S(1)}, s32[8,64]{1,0:T(8,128)}, u32[]{:S(2)}) copy-start(s32[8,64]{1,0:T(8,128)} %mask_ref.1) | copy-start | bytes 6148
  2.4 30.5 %all-to-all-start = ((f32[128,1,2304]{2,1,0:T(1,128)}), f32[128,1,2304]{2,1,0:T(1,128)S(1)}, u32[]{:S(2)}, u32[]{:S(2)}) async-start(f32[128,1,2304]{2,1,0:T(1,128)} %bitcast.11), calls=%async_computation | async-start | bytes 2359296 | tf_op jit(solution)/shard_map/all_to_all | solution.py:230
  13.5 19.3 %copy-start = (bf16[256,256]{1,0:T(8,128)(2,1)S(1)}, bf16[256,256]{1,0:T(8,128)(2,1)}, u32[]{:S(2)}) copy-start(bf16[256,256]{1,0:T(8,128)(2,1)} %constant.21.clone.b_ref) | copy-start | bytes 393220
  13.5 19.3 %copy-start.1 = (bf16[256,256]{1,0:T(8,128)(2,1)S(1)}, bf16[256,256]{1,0:T(8,128)(2,1)}, u32[]{:S(2)}) copy-start(bf16[256,256]{1,0:T(8,128)(2,1)} %constant.20.clone.e_ref) | copy-start | bytes 393220
  13.5 19.3 %copy-start.2 = (bf16[256,256]{1,0:T(8,128)(2,1)S(1)}, bf16[256,256]{1,0:T(8,128)(2,1)}, u32[]{:S(2)}) copy-start(bf16[256,256]{1,0:T(8,128)(2,1)} %constant.19.clone.r_ref) | copy-start | bytes 393220
  13.5 19.3 %copy-start.3 = (bf16[256,256]{1,0:T(8,128)(2,1)S(1)}, bf16[256,256]{1,0:T(8,128)(2,1)}, u32[]{:S(2)}) copy-start(bf16[256,256]{1,0:T(8,128)(2,1)} %constant.18.clone.f_ref) | copy-start | bytes 393220
  13.6 19.3 %copy-start.4 = (f32[64,128]{1,0:T(8,128)S(1)}, f32[64,128]{1,0:T(8,128)}, u32[]{:S(2)}) copy-start(f32[64,128]{1,0:T(8,128)} %constant.23.clone.sin_ref) | copy-start | bytes 98308
  13.6 19.3 %copy-start.5 = (f32[64,128]{1,0:T(8,128)S(1)}, f32[64,128]{1,0:T(8,128)}, u32[]{:S(2)}) copy-start(f32[64,128]{1,0:T(8,128)} %constant.22.clone.cos_ref) | copy-start | bytes 98308
  13.6 20.5 %collective-permute-start = (f32[3,1536]{1,0:T(4,128)S(1)}, f32[3,1536]{1,0:T(4,128)S(1)}, u32[]{:S(2)}, u32[]{:S(2)}) collective-permute-start(f32[3,1536]{1,0:T(4,128)S(1)} %get-tuple-element.16), channel_id=1, source_target_pairs={{0,1},{1,2},{2,3},{3,4},{4,5},{5,6},{6,7},{7,8},{8,9},{9,10},{10,1... | collective-permute-start | bytes 55304 | tf_op jit(solution)/shard_map/ppermute | solution.py:266
  13.7 20.4 %collective-permute-start.1 = (f32[3,1536]{1,0:T(4,128)S(1)}, f32[3,1536]{1,0:T(4,128)S(1)}, u32[]{:S(2)}, u32[]{:S(2)}) collective-permute-start(f32[3,1536]{1,0:T(4,128)S(1)} %get-tuple-element.17), channel_id=1, source_target_pairs={{1,0},{2,1},{3,2},{4,3},{5,4},{6,5},{7,6},{8,7},{9,8},{10,9},{11,1... | collective-permute-start | bytes 55304 | tf_op jit(solution)/shard_map/ppermute | solution.py:267

commit v7 on v6

--- a/solution.py
+++ b/solution.py
@@ -12,7 +12,7 @@
 
 LANES = 128
 AXES = ("y", "z", "x", "core")
-RANKS = ("core", "z", "x", "y")
+RANKS = ("core", "y", "x", "z")
 VMEM_LIMIT = 12 * 2**20
 
 

time: 60.2 us -> 60.1 us (level)
  no operation moved by 1% of the time
where the time goes in v7:
time: 60.1 us; the launch traced here: 59.6 us
  blocking collectives  24.6 us (41%)
  starting transfers between devices  18.4 us (31%)
  waiting for transfers between devices  8.73 us (15%)
  Pallas kernels  7.46 us (12%)
    all_to_all x1, blocking collectives, exchange(): lax.all_to_all(rows.reshape(devices, 1, -1), RANKS, split_axis=0, concat_...  24.6 us
    all_to_all x1, starting transfers between devices, exchange(): lax.all_to_all(rows.reshape(devices, 1, -1), RANKS, split_axis=0, concat_...  11.1 us
    all_to_all x1, waiting for transfers between devices, exchange(): lax.all_to_all(rows.reshape(devices, 1, -1), RANKS, split_axis=0, concat_...  8.73 us
    ppermute x1, starting transfers between devices, body(): lax.ppermute(first, AXES, [((i + 1) % devices, i) for i in range(devices)])  7.16 us
    pallas_call x1, Pallas kernels, body(): pl.pallas_call(functools.partial(forcing_kernel, normal=normal), compiler...  2.76 us
    pallas_call x1, Pallas kernels, body(): pl.pallas_call(pack_kernel, compiler_params=pltpu.CompilerParams(vmem_lim...  2.31 us
  transfers between devices with their start and end apart: 3, of which 1 were waited for; matrix products, arithmetic and copies ran while one was open for 0% of the time, Pallas kernels for 7%

profile of v7, /device:TPU:0, one launch (start us, length us, event | category | flops | bytes accessed | tf_op | source)
XLA Modules:
  0.0 59.6 jit_solution(7282830635825564216)
XLA Ops:
  0.0 2.3 %shard_map.100 = (f32[2304,128]{1,0:T(8,128)}, f32[3,1536]{1,0:T(4,128)S(1)}, f32[3,1536]{1,0:T(4,128)S(1)}) custom-call(f32[3,64,1536]{2,1,0:T(8,128)} %bitcast.9), custom_call_target="tpu_custom_call" | custom-call | tf_op jit(solution)/shard_map/pallas_call | solution.py:252
  2.3 0.0 copy-start.8
  2.3 0.0 copy-start.6
  2.3 0.0 copy-start.7
  2.4 11.1 %all-to-all-start = ((f32[128,1,2304]{2,1,0:T(1,128)}), f32[128,1,2304]{2,1,0:T(1,128)S(1)}, u32[]{:S(2)}, u32[]{:S(2)}) async-start(f32[128,1,2304]{2,1,0:T(1,128)} %bitcast.11), calls=%async_computation | async-start | bytes 2359296 | tf_op jit(solution)/shard_map/all_to_all | solution.py:230
  13.5 0.0 copy-start
  13.5 0.0 copy-start.1
  13.5 0.0 copy-start.2
  13.5 0.0 copy-start.3
  13.6 0.0 copy-start.4
  13.6 0.0 copy-start.5
  13.6 0.1 collective-permute-start
  13.7 7.2 %collective-permute-start.1 = (f32[3,1536]{1,0:T(4,128)S(1)}, f32[3,1536]{1,0:T(4,128)S(1)}, u32[]{:S(2)}, u32[]{:S(2)}) collective-permute-start(f32[3,1536]{1,0:T(4,128)S(1)} %get-tuple-element.17), channel_id=1, source_target_pairs={{1,0},{2,1},{3,2},{4,3},{5,4},{6,5},{7,6},{8,7},{9,8},{10,9},{11,1... | collective-permute-start | bytes 55304 | tf_op jit(solution)/shard_map/ppermute | solution.py:267
  20.8 0.0 copy-done.8
  20.8 0.1 slice_subtract_fusion
  20.9 0.1 broadcast_in_dim_tile.7.slope_ref
  21.0 0.1 broadcast_in_dim_tile.6.flow_ref
  21.1 0.0 copy-done.6
  21.1 0.0 copy-done.7
  21.1 2.8 %shard_map.101 = (f32[3,64,1536]{2,1,0:T(8,128)S(1)}, f32[2,1536]{1,0:T(2,128)S(1)}) custom-call(f32[3,64,1536]{2,1,0:T(8,128)} %bitcast.10, f32[1,1536]{1,0:T(1,128)S(1)} %broadcast_in_dim_tile.6.flow_ref, f32[1,1536]{1,0:T(1,128)S(1)} %broadcast_in_dim_tile.7.slope_ref, s32[8,64]{1,0:T(8,128)S(1)} %copy-done.7, bf16[8,1536]{1,0:T(8,128)(2,1)S(1)} %copy-done.6), custom_call_target="tpu_custom_call" | custom-call | bytes 10000000 | tf_op jit(solution)/shard_map/pallas_call | solution.py:273
  23.9 8.7 %all-to-all-done = f32[128,1,2304]{2,1,0:T(1,128)S(1)} async-done(((f32[128,1,2304]{2,1,0:T(1,128)}), f32[128,1,2304]{2,1,0:T(1,128)S(1)}, u32[]{:S(2)}, u32[]{:S(2)}) %all-to-all-start) | async-done | bytes 1179680 | tf_op jit(solution)/shard_map/all_to_all | solution.py:230
  32.6 0.0 copy-done
  32.6 0.0 copy-done.1
  32.6 0.0 copy-done.2
  32.6 0.0 copy-done.3
  32.6 0.0 copy-done.4
  32.6 0.0 copy-done.5
  32.6 1.2 %shard_map.102 = f32[2304,128]{1,0:T(8,128)S(1)} custom-call(f32[2304,128]{1,0:T(8,128)S(1)} %bitcast.6, bf16[256,256]{1,0:T(8,128)(2,1)S(1)} %copy-done.3, bf16[256,256]{1,0:T(8,128)(2,1)S(1)} %copy-done.2, bf16[256,256]{1,0:T(8,128)(2,1)S(1)} %copy-done.1, bf16[256,256]{1,0:T(8,128)(2,1)S(1)} %copy-done, f32[64,128]{1,0:T(8,128)S(1)} %copy-done.5, ...), custom_call_target="tpu_custom_call" | custom-call | bytes 1000 | tf_op jit(solution)/shard_map/pallas_call | solution.py:281
  33.8 0.0 collective-permute-done.before_ref
  33.8 0.0 collective-permute-done.1.after_ref
  33.8 24.6 %all_to_all.10 = f32[128,1,2304]{2,1,0:T(1,128)S(1)} all-to-all(f32[128,1,2304]{2,1,0:T(1,128)S(1)} %bitcast.7), channel_id=1, replica_groups=mesh['y'=4,'z'=4,'x'=4,'core'=2] {'core','y','x','z'}, dimensions={0} | all-to-all | bytes 2359296 | tf_op jit(solution)/shard_map/all_to_all | solution.py:230
  58.4 1.2 %shard_map.103 = f32[3,64,1536]{2,1,0:T(8,128)} custom-call(f32[2304,128]{1,0:T(8,128)S(1)} %bitcast.8, f32[3,64,1536]{2,1,0:T(8,128)S(1)} %get-tuple-element.14._forcing.f_ref, f32[2,1536]{1,0:T(2,128)S(1)} %get-tuple-element.15._gain.gain_ref, f32[3,1536]{1,0:T(4,128)S(1)} %collective-permute-done.before_ref, f32[3,1536]{1,0:T(4,128)S(1)} %collective-permute-done.1.after_ref), custom_call_target="tpu_custom_call" | custom-call | tf_op jit(solution)/shard_map/pallas_call | solution.py:300
  (2 shorter events, 0.0 us)
Async XLA Ops:
  2.3 18.5 %copy-start.8 = (f32[192]{0:T(256)S(1)}, f32[192]{0:T(256)}, u32[]{:S(2)}) copy-start(f32[192]{0:T(256)} %param.11) | copy-start | bytes 2308
  2.3 18.8 %copy-start.6 = (bf16[8,1536]{1,0:T(8,128)(2,1)S(1)}, bf16[8,1536]{1,0:T(8,128)(2,1)}, u32[]{:S(2)}) copy-start(bf16[8,1536]{1,0:T(8,128)(2,1)} %constant.17.clone.place_ref) | copy-start | bytes 73732
  2.3 18.7 %copy-start.7 = (s32[8,64]{1,0:T(8,128)S(1)}, s32[8,64]{1,0:T(8,128)}, u32[]{:S(2)}) copy-start(s32[8,64]{1,0:T(8,128)} %mask_ref.1) | copy-start | bytes 6148
  2.4 30.2 %all-to-all-start = ((f32[128,1,2304]{2,1,0:T(1,128)}), f32[128,1,2304]{2,1,0:T(1,128)S(1)}, u32[]{:S(2)}, u32[]{:S(2)}) async-start(f32[128,1,2304]{2,1,0:T(1,128)} %bitcast.11), calls=%async_computation | async-start | bytes 2359296 | tf_op jit(solution)/shard_map/all_to_all | solution.py:230
  13.5 19.1 %copy-start = (bf16[256,256]{1,0:T(8,128)(2,1)S(1)}, bf16[256,256]{1,0:T(8,128)(2,1)}, u32[]{:S(2)}) copy-start(bf16[256,256]{1,0:T(8,128)(2,1)} %constant.21.clone.b_ref) | copy-start | bytes 393220
  13.5 19.1 %copy-start.1 = (bf16[256,256]{1,0:T(8,128)(2,1)S(1)}, bf16[256,256]{1,0:T(8,128)(2,1)}, u32[]{:S(2)}) copy-start(bf16[256,256]{1,0:T(8,128)(2,1)} %constant.20.clone.e_ref) | copy-start | bytes 393220
  13.5 19.1 %copy-start.2 = (bf16[256,256]{1,0:T(8,128)(2,1)S(1)}, bf16[256,256]{1,0:T(8,128)(2,1)}, u32[]{:S(2)}) copy-start(bf16[256,256]{1,0:T(8,128)(2,1)} %constant.19.clone.r_ref) | copy-start | bytes 393220
  13.5 19.0 %copy-start.3 = (bf16[256,256]{1,0:T(8,128)(2,1)S(1)}, bf16[256,256]{1,0:T(8,128)(2,1)}, u32[]{:S(2)}) copy-start(bf16[256,256]{1,0:T(8,128)(2,1)} %constant.18.clone.f_ref) | copy-start | bytes 393220
  13.6 19.0 %copy-start.4 = (f32[64,128]{1,0:T(8,128)S(1)}, f32[64,128]{1,0:T(8,128)}, u32[]{:S(2)}) copy-start(f32[64,128]{1,0:T(8,128)} %constant.23.clone.sin_ref) | copy-start | bytes 98308
  13.6 19.0 %copy-start.5 = (f32[64,128]{1,0:T(8,128)S(1)}, f32[64,128]{1,0:T(8,128)}, u32[]{:S(2)}) copy-start(f32[64,128]{1,0:T(8,128)} %constant.22.clone.cos_ref) | copy-start | bytes 98308
  13.6 20.2 %collective-permute-start = (f32[3,1536]{1,0:T(4,128)S(1)}, f32[3,1536]{1,0:T(4,128)S(1)}, u32[]{:S(2)}, u32[]{:S(2)}) collective-permute-start(f32[3,1536]{1,0:T(4,128)S(1)} %get-tuple-element.16), channel_id=1, source_target_pairs={{0,1},{1,2},{2,3},{3,4},{4,5},{5,6},{6,7},{7,8},{8,9},{9,10},{10,1... | collective-permute-start | bytes 55304 | tf_op jit(solution)/shard_map/ppermute | solution.py:266
  13.7 20.2 %collective-permute-start.1 = (f32[3,1536]{1,0:T(4,128)S(1)}, f32[3,1536]{1,0:T(4,128)S(1)}, u32[]{:S(2)}, u32[]{:S(2)}) collective-permute-start(f32[3,1536]{1,0:T(4,128)S(1)} %get-tuple-element.17), channel_id=1, source_target_pairs={{1,0},{2,1},{3,2},{4,3},{5,4},{6,5},{7,6},{8,7},{9,8},{10,9},{11,1... | collective-permute-start | bytes 55304 | tf_op jit(solution)/shard_map/ppermute | solution.py:267
